TPU v7x, 32 devices: a whole 2x2x4 slice. The times are simulated.
32 devices in a mesh: row: 8 (over z, y), col: 4 (over x, core).
Axes of the slice: x: 2, y: 2, z: 4, core: 2. Of those that a mesh axis runs over, the one named last changes fastest.
Arguments:
- orbitals: bfloat16 [32, 64000], P(('row', 'col')), may hold values from -6 to 6
- pair_list: int32 [32, 8, 2], P(('row', 'col')), may hold values from 0 to 7, as said below
- pair_count: int32 [32], P(('row', 'col')), may hold values from 1 to 8
Outputs:
- exchange_fields: float32 [32, 64000], P(('row', 'col'))
Inputs may be any that keep to these rules, and one draw needn't show every extreme that they name: pair_list[., ., 0] is below 4 and pair_list[., ., 1] below 8.
All inputs are finite; a program needn't handle non-finite values.
Results may differ from a plain program's by a relative error of at most 0.0004.
Values may be sent and summed in bfloat16 or wider, within the bound.
No kernel may reach another device: no remote copies, remote signals or barrier semaphores. Data moves between devices by JAX's collectives and lax.ppermute only.
A program may use at most 64 MiB of HBM per device.

v0:
```python
import jax
import jax.numpy as jnp
from jax import lax
from jax.sharding import PartitionSpec as P

GX = 40


screen_width = 0.9
axis_forms = ("kx,xyz->kyz", "ky,xyz->xkz", "kz,xyz->xyk")


def contract(pattern, operator, values):
    return jnp.einsum(
        pattern,
        operator,
        values,
        precision=lax.Precision.HIGHEST,
        preferred_element_type=jnp.float32,
    )


def dft_tables(length):
    counter = lax.iota(jnp.int32, length)
    phases = (counter[:, None] * counter[None, :] % length).astype(jnp.float32) * (
        2.0 * jnp.pi / length
    )
    frequency = jnp.where(counter < length // 2, counter, counter - length).astype(jnp.float32) * (
        2.0 * jnp.pi / length
    )
    squared = frequency * frequency
    squared_sum = squared[:, None, None] + squared[None, :, None] + squared[None, None, :]
    safe_sum = jnp.where(squared_sum > 0, squared_sum, 1.0)
    screened = 4.0 * jnp.pi * (1.0 - jnp.exp(-safe_sum / (4.0 * screen_width**2))) / safe_sum
    kernel = jnp.where(squared_sum > 0, screened, jnp.pi / screen_width**2)
    return (jnp.cos(phases), jnp.sin(phases), kernel)


def solve_potential(density, cosine_table, sine_table, kernel):
    length = density.shape[0]
    real_part = contract(axis_forms[0], cosine_table, density)
    imag_part = -contract(axis_forms[0], sine_table, density)
    for pattern in axis_forms[1:]:
        real_part, imag_part = (
            contract(pattern, cosine_table, real_part) + contract(pattern, sine_table, imag_part),
            contract(pattern, cosine_table, imag_part) - contract(pattern, sine_table, real_part),
        )
    real_part = real_part * kernel
    imag_part = imag_part * kernel
    for pattern in axis_forms[:2]:
        real_part, imag_part = (
            contract(pattern, cosine_table, real_part) - contract(pattern, sine_table, imag_part),
            contract(pattern, sine_table, real_part) + contract(pattern, cosine_table, imag_part),
        )
    real_part = contract(axis_forms[2], cosine_table, real_part) - contract(
        axis_forms[2], sine_table, imag_part
    )
    return real_part / float(length**3)


def set_row(terms_block, slot, values):
    return lax.dynamic_update_index_in_dim(terms_block, values[None, :], slot, 0)


def collect_rows(band_rows, terms_block, count):
    wanted = lax.iota(jnp.int32, count)
    selector = (wanted[:, None] == band_rows[None, :]).astype(jnp.float32)
    return jnp.dot(
        selector, terms_block, precision=lax.Precision.HIGHEST, preferred_element_type=jnp.float32
    )


def shards(orbitals, pair_list, pair_count):
    per_device = orbitals.shape[0]
    grid_size = orbitals.shape[1]
    column_count = lax.axis_size("col")
    row_index = lax.axis_index("row")
    col_index = lax.axis_index("col")
    first_local = pair_list[0, :, 0]
    second_local = pair_list[0, :, 1]
    pair_total = pair_count[0]
    slot_count = pair_list.shape[1]
    first_global = row_index * (per_device * column_count) + first_local
    second_global = (
        second_local // per_device * column_count + col_index
    ) * per_device + second_local % per_device
    distinct = jnp.where(first_global != second_global, 1.0, 0.0).astype(jnp.float32)
    cosine_table, sine_table, kernel = dft_tables(GX)
    column_block = lax.all_gather(orbitals, "row", axis=0, tiled=True)
    empty_terms = jnp.zeros((slot_count, grid_size), jnp.float32)

    def pair_terms(terms, pair_slot, first_wave):
        first_terms, second_terms = terms
        second_row = second_local[pair_slot]
        second_wave = lax.dynamic_index_in_dim(column_block, second_row, 0, keepdims=False).astype(
            jnp.float32
        )
        density = (first_wave * second_wave).reshape(GX, GX, GX)
        potential = solve_potential(density, cosine_table, sine_table, kernel).reshape(-1)
        first_terms = set_row(first_terms, pair_slot, potential * second_wave)
        second_terms = set_row(
            second_terms, pair_slot, distinct[pair_slot] * potential * first_wave
        )
        return (first_terms, second_terms)

    row_block = lax.all_gather(orbitals, "col", axis=0, tiled=True)

    def visit_pair(pair_slot, terms):
        first_row = first_local[pair_slot]
        first_wave = lax.dynamic_index_in_dim(row_block, first_row, 0, keepdims=False).astype(
            jnp.float32
        )
        return pair_terms(terms, pair_slot, first_wave)

    first_terms, second_terms = lax.fori_loop(0, pair_total, visit_pair, (empty_terms, empty_terms))
    first_rows_total = per_device * column_count
    second_rows_total = column_block.shape[0]
    first_fields = collect_rows(first_local, first_terms, first_rows_total)
    second_fields = collect_rows(second_local, second_terms, second_rows_total)
    own_first = lax.psum_scatter(first_fields, "col", scatter_dimension=0, tiled=True)
    own_second = lax.psum_scatter(second_fields, "row", scatter_dimension=0, tiled=True)
    return own_first + own_second


def solution(mesh):
    return jax.shard_map(
        shards,
        mesh=mesh,
        in_specs=(P(("row", "col"), None), P(("row", "col"), None, None), P(("row", "col"))),
        out_specs=P(("row", "col"), None),
        check_vma=False,
    )
```

profile of v0, /device:TPU:0, one launch (start us, length us, event | category | flops | bytes accessed | tf_op | source)
XLA Modules:
  0.0 601.8 jit_solution(2561269353833744239)
XLA Ops:
  6.5 46.2 %all-gather.1 = bf16[8,1,64000]{2,1,0:T(2,128)(2,1)} all-gather(bf16[1,1,64000]{2,1,0:T(2,128)(2,1)} %bitcast.204), channel_id=1, replica_groups=mesh['row'=8,'col'=4] {'row'}, dimensions={0}, use_global_device_ids=true | all-gather | bytes 1152000 | tf_op jit(solution)/shard_map/all_gather | solution.py:89
  52.8 9.9 %all-gather = bf16[4,1,64000]{2,1,0:T(2,128)(2,1)S(1)} all-gather(bf16[1,1,64000]{2,1,0:T(2,128)(2,1)S(1)} %bitcast.205), channel_id=1, replica_groups=mesh['row'=8,'col'=4] {'col'}, dimensions={0}, use_global_device_ids=true | all-gather | bytes 640000 | tf_op jit(solution)/shard_map/all_gather | solution.py:106
  68.4 381.3 %while.14 = (s32[]{:T(128)}, f32[8,64000]{1,0:T(8,128)}, f32[8,64000]{1,0:T(8,128)}, s32[]{:T(128)}, s32[8]{0:T(128)S(1)}, /*index=5*/bf16[4,64000]{1,0:T(4,128)...) while((s32[]{:T(128)}, f32[8,64000]{1,0:T(8,128)}, ...), condition=%wide.region_1.2_spmd.clone.clone, body=%wide.region_0.1_spmd.clone.clone.sunk | while | flops 617184000 | bytes 27917484 | solution.py:115
  101.8 2.2 multiply_multiply_fusion.2
  104.0 6.0 dynamic_update_slice.14
  110.0 5.9 dynamic_update_slice.13
  149.3 2.2 multiply_multiply_fusion.2
  151.5 6.0 dynamic_update_slice.14
  157.5 5.9 dynamic_update_slice.13
  196.9 2.2 multiply_multiply_fusion.2
  199.1 6.0 dynamic_update_slice.14
  205.1 5.9 dynamic_update_slice.13
  244.4 2.2 multiply_multiply_fusion.2
  246.7 6.0 dynamic_update_slice.14
  252.6 5.9 dynamic_update_slice.13
  292.0 2.2 multiply_multiply_fusion.2
  294.2 6.0 dynamic_update_slice.14
  300.2 5.9 dynamic_update_slice.13
  339.6 2.2 multiply_multiply_fusion.2
  341.8 6.0 dynamic_update_slice.14
  347.8 5.9 dynamic_update_slice.13
  387.1 2.2 multiply_multiply_fusion.2
  389.3 6.0 dynamic_update_slice.14
  395.3 5.9 dynamic_update_slice.13
  434.7 2.2 multiply_multiply_fusion.2
  436.9 6.0 dynamic_update_slice.14
  442.9 5.9 dynamic_update_slice.13
  449.7 3.8 fusion.201
  453.6 2.3 fusion.199
  457.7 27.9 %all-reduce.5.cloned.1.call-done = f32[4,64000]{1,0:T(4,128)} async-done(((f32[4,64000]{1,0:T(4,128)}), f32[4,64000]{1,0:T(4,128)}) %all-reduce.5.cloned.1.call-update) | async-done | bytes 1024016
  485.6 105.2 %all-reduce.7.cloned.1.call-done = f32[8,64000]{1,0:T(8,128)} async-done(((f32[8,64000]{1,0:T(8,128)}), f32[8,64000]{1,0:T(8,128)}) %all-reduce.7.cloned.1.call-update) | async-done | bytes 2048016
  590.9 4.1 dynamic-slice_add_fusion
  (320 shorter events, 240.8 us)
Async XLA Ops:
  6.5 46.2 %copy-start.3 = (bf16[1,64000]{1,0:T(2,128)(2,1)S(1)}, bf16[1,64000]{1,0:T(2,128)(2,1)}, u32[]{:S(2)}) copy-start(bf16[1,64000]{1,0:T(2,128)(2,1)} %param.5) | copy-start | bytes 384004
  6.5 56.1 %copy-start.4 = (s32[1,8,2]{1,2,0:T(2,128)S(1)}, s32[1,8,2]{1,2,0:T(2,128)}, u32[]{:S(2)}) copy-start(s32[1,8,2]{1,2,0:T(2,128)} %param.6) | copy-start | bytes 196
  6.5 479.1 %all-reduce.5.cloned.1.call-start = ((), (), s32[]{:S(2)}) async-start(), calls=%async_computation | async-start | bytes 2048000
  69.0 6.8 %copy-start = (bf16[8,64000]{1,0:T(8,128)(2,1)}, bf16[8,64000]{1,0:T(8,128)(2,1)S(1)}, u32[]{:S(2)}) copy-start(bf16[8,64000]{1,0:T(8,128)(2,1)S(1)} %get-tuple-element.343) | copy-start | bytes 3072004 | tf_op jit(solution)/shard_map/while
  99.0 2.8 copy-start.1
  116.6 6.8 %copy-start = (bf16[8,64000]{1,0:T(8,128)(2,1)}, bf16[8,64000]{1,0:T(8,128)(2,1)S(1)}, u32[]{:S(2)}) copy-start(bf16[8,64000]{1,0:T(8,128)(2,1)S(1)} %get-tuple-element.343) | copy-start | bytes 3072004 | tf_op jit(solution)/shard_map/while
  146.5 2.8 copy-start.1
  164.1 6.8 %copy-start = (bf16[8,64000]{1,0:T(8,128)(2,1)}, bf16[8,64000]{1,0:T(8,128)(2,1)S(1)}, u32[]{:S(2)}) copy-start(bf16[8,64000]{1,0:T(8,128)(2,1)S(1)} %get-tuple-element.343) | copy-start | bytes 3072004 | tf_op jit(solution)/shard_map/while
  194.1 2.8 copy-start.1
  211.7 6.8 %copy-start = (bf16[8,64000]{1,0:T(8,128)(2,1)}, bf16[8,64000]{1,0:T(8,128)(2,1)S(1)}, u32[]{:S(2)}) copy-start(bf16[8,64000]{1,0:T(8,128)(2,1)S(1)} %get-tuple-element.343) | copy-start | bytes 3072004 | tf_op jit(solution)/shard_map/while
  241.6 2.8 copy-start.1
  259.3 6.8 %copy-start = (bf16[8,64000]{1,0:T(8,128)(2,1)}, bf16[8,64000]{1,0:T(8,128)(2,1)S(1)}, u32[]{:S(2)}) copy-start(bf16[8,64000]{1,0:T(8,128)(2,1)S(1)} %get-tuple-element.343) | copy-start | bytes 3072004 | tf_op jit(solution)/shard_map/while
  289.2 2.8 copy-start.1
  306.8 6.8 %copy-start = (bf16[8,64000]{1,0:T(8,128)(2,1)}, bf16[8,64000]{1,0:T(8,128)(2,1)S(1)}, u32[]{:S(2)}) copy-start(bf16[8,64000]{1,0:T(8,128)(2,1)S(1)} %get-tuple-element.343) | copy-start | bytes 3072004 | tf_op jit(solution)/shard_map/while
  336.8 2.8 copy-start.1
  354.4 6.8 %copy-start = (bf16[8,64000]{1,0:T(8,128)(2,1)}, bf16[8,64000]{1,0:T(8,128)(2,1)S(1)}, u32[]{:S(2)}) copy-start(bf16[8,64000]{1,0:T(8,128)(2,1)S(1)} %get-tuple-element.343) | copy-start | bytes 3072004 | tf_op jit(solution)/shard_map/while
  384.3 2.8 copy-start.1
  401.9 6.8 %copy-start = (bf16[8,64000]{1,0:T(8,128)(2,1)}, bf16[8,64000]{1,0:T(8,128)(2,1)S(1)}, u32[]{:S(2)}) copy-start(bf16[8,64000]{1,0:T(8,128)(2,1)S(1)} %get-tuple-element.343) | copy-start | bytes 3072004 | tf_op jit(solution)/shard_map/while
  431.9 2.8 copy-start.1
  449.7 3.9 copy-start.2
  453.5 137.4 %all-reduce.7.cloned.1.call-start = ((), (), s32[]{:S(2)}) async-start(), calls=%async_computation.1 | async-start | bytes 4096000
  455.9 0.7 copy-start.6
  455.9 1.3 copy-start.5
Sparse Core Ops, SparseCore 0:
  453.6 31.9 all-reduce.4
  489.7 101.1 all-reduce.6
where the time goes:
time: 605 us; the launch traced here: 602 us
  matrix products  179 us (30%)
  local copies, waits for them, and re-layouts  147 us (24%)
  waiting for transfers between devices  133 us (22%)
  blocking collectives  56.1 us (9%)
  other arithmetic  38.3 us (6%)
  loops' own time  35 us (6%)
  between operations  13.4 us (2%)
    dot_general x160, matrix products, contract(): jnp.einsum(pattern, operator, values, precision=lax.Precision.HIGHEST, pr...  173 us
    unnamed x4, waiting for transfers between devices  133 us
    dynamic_update_slice x16, local copies, waits for them, and re-layouts, set_row(): lax.dynamic_update_index_in_dim(terms_block, values[None, :], slot, 0)  95.5 us
    all_gather x1, blocking collectives, shards(): column_block = lax.all_gather(orbitals, 'row', axis=0, tiled=True)  46.2 us
    another operation x1, loops' own time, shards(): lax.fori_loop(0, pair_total, visit_pair, (empty_terms, empty_terms))  35 us
    mul x8, other arithmetic, pair_terms(): distinct[pair_slot] * potential * first_wave  17.7 us
    mul x8, other arithmetic, pair_terms(): density = (first_wave * second_wave).reshape(GX, GX, GX)  16.4 us
  transfers between devices with their start and end apart: 2, of which 2 were waited for; matrix products, arithmetic and copies ran while one was open for 1% of the time, Pallas kernels for 0%

commit v1 on v0

v1 whole, which is shorter than its diff:
```python
import functools

import jax
import jax.numpy as jnp
import ml_dtypes
import numpy as np
from jax import lax
from jax.experimental import pallas as pl
from jax.experimental.pallas import tpu as pltpu
from jax.sharding import PartitionSpec as P

GX = 40
LANES = 128
SIDE = 3
THIRD = -(-GX // SIDE)
PACK = THIRD * GX
ROWS = SIDE * PACK
LIVE = GX * GX
SPARE = SIDE * GX
DUO = 2 * GX
QUAD = 4 * GX
GROUP = 5
VMEM_LIMIT = 48 * 1024 * 1024
screen_width = 0.9
F32 = jnp.float32
BF16 = jnp.bfloat16


def real_basis():
    half = GX // 2
    point = np.arange(GX)
    rows = [np.cos(2 * np.pi * (k * point % GX) / GX) for k in range(half + 1)]
    rows += [np.sin(2 * np.pi * (k * point % GX) / GX) for k in range(1, half)]
    frequency = np.concatenate([np.arange(half + 1), np.arange(1, half)])
    norm = np.where((frequency == 0) | (frequency == half), 1.0, 2.0) / GX
    return np.stack(rows), frequency, norm


def halves(table):
    high = table.astype(ml_dtypes.bfloat16)
    low = (table - high.astype(np.float64)).astype(ml_dtypes.bfloat16)
    return high, low


def left_table(table):
    high, low = halves(np.kron(np.eye(2), table))
    return np.concatenate([high, low, high], axis=1)


def right_table(table):
    wide = np.zeros((LANES, LANES))
    for p in range(SIDE):
        wide[p * GX : (p + 1) * GX, p * GX : (p + 1) * GX] = table
    high, low = halves(wide)
    both = np.concatenate([high, low], axis=1)
    return np.concatenate([both, both], axis=0)


def kernel_table():
    _, frequency, norm = real_basis()
    wave = frequency * (2.0 * np.pi / GX)
    squared = wave * wave
    total = squared[:, None, None] + squared[None, :, None] + squared[None, None, :]
    safe = np.where(total > 0, total, 1.0)
    screened = 4.0 * np.pi * (1.0 - np.exp(-safe / (4.0 * screen_width**2))) / safe
    kernel = np.where(total > 0, screened, np.pi / screen_width**2)
    kernel = kernel * norm[:, None, None] * norm[None, :, None] * norm[None, None, :]
    rows = np.swapaxes(kernel, 0, 1).reshape(LIVE, GX)
    out = np.zeros((LIVE, LANES), np.float32)
    for p in range(SIDE):
        out[:, p * GX : (p + 1) * GX] = rows
    return out


def place(out, row, col):
    for z in range(GX):
        out[row + z, col + z] = 1.0


def pack_table():
    out = np.zeros((SIDE, GX, LANES), np.float32)
    for third in range(SIDE):
        place(out[third], 0, third * GX)
    return out.astype(ml_dtypes.bfloat16)


def spread_table():
    out = np.zeros((SIDE * LANES, SIDE * LANES), np.float32)
    for third in range(SIDE):
        for p in range(SIDE):
            place(out, p * LANES + third * GX, third * LANES + p * GX)
    return out.astype(ml_dtypes.bfloat16)


def repeat_table():
    out = np.zeros((LANES, SIDE * LANES), np.float32)
    for third in range(SIDE):
        for p in range(SIDE):
            place(out, third * GX, third * LANES + p * GX)
    return out.astype(ml_dtypes.bfloat16)


def dot(a, b):
    return jnp.dot(a, b, preferred_element_type=F32)


def split(values):
    high = values.astype(BF16)
    return high, (values - high.astype(F32)).astype(BF16)


def contract_rows(table, values):
    high, low = split(values)
    return dot(table, jnp.concatenate([high, high, low], axis=0))


def contract_lanes(values, table):
    both = dot(jnp.concatenate(split(values), axis=1), table)
    return both[:, :LANES] + both[:, LANES:]


def fold(values):
    return jnp.concatenate([values[:DUO], values[DUO:]], axis=1)


def unfold(values):
    return jnp.concatenate([values[:, :LANES], values[:, LANES:]], axis=0)


def in_groups(body):
    def group(outer, carry):
        body([outer * GROUP + inner for inner in range(GROUP)])
        return carry

    lax.fori_loop(0, GX // 4 // GROUP, group, 0)


def quad(step):
    return pl.ds(step * QUAD, QUAD)


def load_planes(ref, step):
    planes = [ref[pl.ds(step * 4 + i, GX, stride=GX), :] for i in range(4)]
    left = jnp.concatenate(planes[:2], axis=0)
    return jnp.concatenate([left, jnp.concatenate(planes[2:], axis=0)], axis=1)


def store_planes(ref, step, values):
    for i in range(4):
        rows, lanes = i % 2 * GX, i // 2 * LANES
        ref[pl.ds(step * 4 + i, GX, stride=GX), :] = values[rows : rows + GX, lanes : lanes + LANES]


def count_vector(list_ref, count_ref, first_row):
    row = lax.broadcasted_iota(jnp.int32, (8, LANES), 0) - first_row
    lane = lax.broadcasted_iota(jnp.int32, (8, LANES), 1) - SPARE
    counts = jnp.zeros((8, LANES), F32)
    for p in range(list_ref.shape[1]):
        here = (row == list_ref[0, p, 0]) & (lane == list_ref[0, p, 1])
        live = jnp.where(p < count_ref[0], 1.0, 0.0)
        counts = counts + jnp.where(here, live, 0.0)
    return counts


def pack_kernel(col_total, band_ref, table_ref, *rest):
    out_ref = rest[-1]
    total = None
    for third in range(SIDE):
        rows = min(PACK, LIVE - third * PACK)
        piece = dot(band_ref[pl.ds(third * PACK, rows), :], table_ref[third])
        if rows < PACK:
            piece = jnp.concatenate([piece, jnp.zeros((PACK - rows, LANES), F32)], axis=0)
        total = piece if total is None else total + piece
    if len(rest) > 1:
        counts = count_vector(rest[0], rest[1], 0) + count_vector(rest[2], rest[3], col_total)
        empty = jnp.zeros((PACK - counts.shape[0], LANES), F32)
        total = total + jnp.concatenate([counts, empty], axis=0)
    out_ref[...] = total.astype(BF16)


def spread_waves(own_bands, repeat_ref, wave_refs):
    for band, wave_ref in zip(own_bands, wave_refs):
        wide = dot(band, repeat_ref[...])
        for third in range(SIDE):
            wave_ref[pl.ds(third * PACK, PACK), :] = wide[:, third * LANES : (third + 1) * LANES]


def solve_pairs(total, lists, load_band, tables, out_refs, scratch):
    spread_ref, repeat_ref, z_ref, z_back_ref, row_ref, row_back_ref, kernel_ref = tables
    trio_ref, *wave_refs, partner_ref, work_ref, work2_ref, sum0_ref, sum1_ref = scratch
    sum_refs = (sum0_ref, sum1_ref)
    slot_list, band_list, weight_list = lists
    for sum_ref in sum_refs:
        sum_ref[...] = jnp.zeros_like(sum_ref)
    side = lax.broadcasted_iota(jnp.int32, (1, LANES), 1) // GX

    def by_side(values):
        row = jnp.zeros((1, LANES), F32)
        for p in range(SIDE):
            row = jnp.where(side == p, values[p].astype(F32), row)
        return row

    def trio(at, carry):
        places = [at * SIDE + p for p in range(SIDE)]
        for p, place in enumerate(places):
            load_band(slot_list[place], trio_ref, p)
        bands = [band_list[place] for place in places]
        weights = [weight_list[place] for place in places]
        is_mate = by_side(bands) > 0.5
        scales = [
            by_side([jnp.where(bands[p] == which, weights[p], 0) for p in range(SIDE)])
            for which in range(2)
        ]
        wide = dot(trio_ref[...], spread_ref[...])
        for third in range(SIDE):
            partner_ref[pl.ds(third * PACK, PACK), :] = wide[:, third * LANES : (third + 1) * LANES]

        def forward(steps):
            values = []
            for step in steps:
                wave = jnp.where(is_mate, wave_refs[1][quad(step), :], wave_refs[0][quad(step), :])
                values.append(partner_ref[quad(step), :] * wave)
            values = [contract_lanes(v, z_ref[...]) for v in values]
            values = [contract_rows(row_ref[...], fold(v)) for v in values]
            for step, v in zip(steps, values):
                work_ref[quad(step), :] = unfold(v)

        def across(steps):
            values = [load_planes(work_ref, step) for step in steps]
            values = [contract_rows(row_ref[...], v) for v in values]
            values = [v * fold(kernel_ref[quad(step), :]) for step, v in zip(steps, values)]
            values = [contract_rows(row_back_ref[...], v) for v in values]
            for step, v in zip(steps, values):
                store_planes(work2_ref, step, v)

        def back(steps):
            values = [fold(work2_ref[quad(step), :]) for step in steps]
            values = [unfold(contract_rows(row_back_ref[...], v)) for v in values]
            values = [contract_lanes(v, z_back_ref[...]) for v in values]
            for step, v in zip(steps, values):
                v = v * partner_ref[quad(step), :]
                for sum_ref, scale in zip(sum_refs, scales):
                    sum_ref[quad(step), :] = sum_ref[quad(step), :] + v * scale

        for phase in (forward, across, back):
            in_groups(phase)
        return carry

    lax.fori_loop(0, (total + SIDE - 1) // SIDE, trio, 0)

    def pack_sums(step, carry):
        for out_ref, sum_ref in zip(out_refs, sum_refs):
            packed = jnp.zeros((GX, LANES), F32)
            for third in range(SIDE):
                values = sum_ref[pl.ds(third * PACK + step * GX, GX), :]
                field = jnp.zeros((GX, LANES), F32)
                for p in range(SIDE):
                    shift = (third - p) * GX % LANES
                    field = field + (pltpu.roll(values, shift, 1) if shift else values)
                packed = jnp.where(side == third, field, packed)
            out_ref[pl.ds(step * GX, GX), :] = packed
        return carry

    lax.fori_loop(0, THIRD, pack_sums, 0)


def near_kernel(row_total, col_total, *refs):
    pairs_wide = col_total // 2
    slots = row_total * pairs_wide
    band_refs, refs = refs[:slots], refs[slots:]
    mate_ref, tables, out_refs, refs = refs[0], refs[1:8], refs[8:10], refs[10:]
    (count_vmem, count_smem, slot_list, band_list, weight_list), refs = refs[:5], refs[5:]
    scratch, sem = refs[:-1], refs[-1]

    lane = lax.broadcasted_iota(jnp.int32, (8, LANES), 1)
    counts = jnp.zeros((8, LANES), F32)
    for s in range(slots):
        spare = band_refs[s][0:16, :].astype(F32)[0:8]
        shift = (s * row_total - SPARE) % LANES
        moved = pltpu.roll(spare, shift, 1) if shift else spare
        counts = jnp.where(lane // row_total == s, moved, counts)
    count_vmem[...] = counts.astype(jnp.int32)
    copy = pltpu.make_async_copy(count_vmem, count_smem, sem)
    copy.start()
    spread_waves((band_refs[0][...], mate_ref[...]), tables[1], scratch[1:3])
    copy.wait()
    row = lax.axis_index("row")
    col = lax.axis_index("col")
    total = jnp.int32(0)
    for which in range(2):
        mine = col ^ which
        for slot in range(slots):
            row_flip, x_flip = slot // pairs_wide, slot % pairs_wide
            other_row = row ^ row_flip
            other_col = col ^ (2 * x_flip)
            weight = count_smem[mine, x_flip * row_total + other_row]
            if which or slot:
                mirror_lane = row_flip * pairs_wide * row_total + row
                weight = weight + count_smem[which * col_total + other_col, mirror_lane]
            slot_list[total] = slot
            band_list[total] = which
            weight_list[total] = weight
            total = total + jnp.where(weight > 0, 1, 0)
    lists = (slot_list, band_list, weight_list)
    for p in range(SIDE - 1):
        slot_list[total + p] = 0
        band_list[total + p] = 0
        weight_list[total + p] = 0

    def load_band(place, target, p):
        for s in range(slots):

            @pl.when(place == s)
            def _():
                target[:, p * LANES : (p + 1) * LANES] = band_refs[s][...]

    solve_pairs(total, lists, load_band, tables, out_refs, scratch)


def far_kernel(total_ref, slot_list, band_list, weight_list, bands_ref, own_ref, mate_ref, *refs):
    tables, out_refs, refs = refs[:7], refs[7:9], refs[9:]
    buffer, scratch = refs[0], refs[1:]
    spread_waves((own_ref[...], mate_ref[...]), tables[1], scratch[1:3])

    def load_band(place, target, p):
        pltpu.sync_copy(bands_ref.at[place], buffer)
        target[:, p * LANES : (p + 1) * LANES] = buffer[...]

    lists = (slot_list, band_list, weight_list)
    solve_pairs(total_ref[0], lists, load_band, tables, out_refs, scratch)


def finish_kernel(own_ref, part_ref, out_ref):
    for third in range(SIDE):
        rows = min(PACK, LIVE - third * PACK)
        values = own_ref[pl.ds(0, rows), :] + part_ref[pl.ds(0, rows), :]
        if third:
            values = pltpu.roll(values, LANES - third * GX, 1)
        out_ref[pl.ds(third * PACK, rows), :] = values[:, :GX]


VMEM_SPEC = pl.BlockSpec(memory_space=pltpu.VMEM)
SMEM_SPEC = pl.BlockSpec(memory_space=pltpu.SMEM)
ANY_SPEC = pl.BlockSpec(memory_space=pl.ANY)
PARAMS = pltpu.CompilerParams(vmem_limit_bytes=VMEM_LIMIT)


def solve_tables():
    basis, _, _ = real_basis()
    return [
        spread_table(),
        repeat_table(),
        right_table(basis.T),
        right_table(basis),
        left_table(basis),
        left_table(basis.T),
        kernel_table(),
    ]


def solve_scratch():
    wide = pltpu.VMEM((ROWS, LANES), F32)
    return [pltpu.VMEM((PACK, SIDE * LANES), BF16)] + [wide] * 7


def field_shapes():
    return [jax.ShapeDtypeStruct((PACK, LANES), F32)] * 2


def swap(values, axis, size, flip):
    return lax.ppermute(values, axis, [(i, i ^ flip) for i in range(size)])


def count_pairs(pair_list, pair_count, row_total, col_total):
    slots = pair_list.shape[1]
    live = lax.iota(jnp.int32, slots) < pair_count[0]
    first = pair_list[0, :, 0][:, None, None] == lax.iota(jnp.int32, col_total)[None, :, None]
    second = pair_list[0, :, 1][:, None, None] == lax.iota(jnp.int32, row_total)[None, None, :]
    return jnp.sum((first & second & live[:, None, None]).astype(F32), axis=0)


def pack_band(orbitals, col_total, extras):
    return pl.pallas_call(
        functools.partial(pack_kernel, col_total),
        out_shape=jax.ShapeDtypeStruct((PACK, LANES), BF16),
        in_specs=[VMEM_SPEC] * 2 + [SMEM_SPEC] * len(extras),
        out_specs=VMEM_SPEC,
        compiler_params=PARAMS,
        name="pack_band",
    )(orbitals.reshape(LIVE, GX), jnp.asarray(pack_table()), *extras)


def finish(own, part):
    field = pl.pallas_call(
        finish_kernel,
        out_shape=jax.ShapeDtypeStruct((LIVE, GX), F32),
        in_specs=[VMEM_SPEC] * 2,
        out_specs=VMEM_SPEC,
        compiler_params=PARAMS,
        name="add_parts",
    )(own, part)
    return field.reshape(1, LIVE * GX)


def near_shards(row_total, col_total, orbitals, pair_list, pair_count):
    row_swap = lambda values, flip: swap(values, "row", row_total, flip)
    col_swap = lambda values, flip: swap(values, "col", col_total, flip)
    extras = (pair_list, pair_count, col_swap(pair_list, 1), col_swap(pair_count, 1))
    own = pack_band(orbitals, col_total, extras)
    wide = col_total // 2
    bands = {(0, 0, 0): own}
    for z in range(1, row_total // 2):
        bands[z, 0, 0] = row_swap(own, 2 * z)
    for z in range(row_total // 2):
        for x in range(1, wide):
            bands[z, 0, x] = col_swap(bands[z, 0, 0], 2 * x)
        bands[z, 1, 0] = row_swap(bands[z, 0, 0], 1)
    for z in range(row_total // 2):
        for x in range(1, wide):
            if z % 2:
                bands[z, 1, x] = col_swap(bands[z, 1, 0], 2 * x)
            else:
                bands[z, 1, x] = row_swap(bands[z, 0, x], 1)
    mate = col_swap(own, 1)
    slots = row_total * wide
    ordered = [
        bands[s // wide // 2, s // wide % 2, s % wide] for s in range(slots)
    ]
    places = 2 * slots + SIDE
    fields = pl.pallas_call(
        functools.partial(near_kernel, row_total, col_total),
        out_shape=field_shapes(),
        in_specs=[VMEM_SPEC] * (slots + 8),
        out_specs=[VMEM_SPEC] * 2,
        scratch_shapes=[
            pltpu.VMEM((8, LANES), jnp.int32),
            pltpu.SMEM((8, LANES), jnp.int32),
            pltpu.SMEM((places,), jnp.int32),
            pltpu.SMEM((places,), jnp.int32),
            pltpu.SMEM((places,), jnp.int32),
        ]
        + solve_scratch()
        + [pltpu.SemaphoreType.DMA],
        compiler_params=PARAMS,
        name="solve_pairs",
    )(*ordered, mate, *map(jnp.asarray, solve_tables()))
    return finish(fields[0], col_swap(fields[1], 1))


def far_shards(row_total, col_total, orbitals, pair_list, pair_count):
    counts = count_pairs(pair_list, pair_count, row_total, col_total)
    own = pack_band(orbitals, col_total, ())
    axes = ("row", "col")
    table = lax.all_gather(counts.reshape(-1), axes)
    table = table.reshape(row_total, col_total, col_total, row_total)
    wide = col_total // 2
    column = lax.all_gather(own, "row")
    columns = [column] + [swap(column, "col", col_total, 2 * x) for x in range(1, wide)]
    bands = jnp.concatenate(columns, axis=0)
    row = lax.axis_index("row")
    col = lax.axis_index("col")
    mine = jnp.stack([col, col ^ 1])
    other_col = ((col // 2) ^ lax.iota(jnp.int32, wide)) * 2 + col % 2
    other_row = lax.iota(jnp.int32, row_total)
    direct = table[row][other_col][:, mine]
    direct = jnp.transpose(direct, (1, 2, 0))
    mirror = table[:, :, :, row][:, mine][:, :, other_col]
    mirror = jnp.transpose(mirror, (1, 0, 2))
    same = (mine[:, None, None] == other_col[None, None, :]) & (other_row == row)[None, :, None]
    weights = (direct + jnp.where(same, 0.0, mirror)).astype(jnp.int32).reshape(-1)
    index = lax.iota(jnp.int32, weights.shape[0])
    order = jnp.argsort(jnp.where(weights > 0, 0, 1), stable=True)
    pad = lambda values: jnp.pad(values.astype(jnp.int32), (0, SIDE))
    slots = row_total * wide
    slot = order % slots
    band = (slot % wide) * row_total + slot // wide
    total = jnp.sum((weights > 0).astype(jnp.int32)).reshape(1)
    fields = pl.pallas_call(
        far_kernel,
        out_shape=field_shapes(),
        in_specs=[SMEM_SPEC] * 4 + [ANY_SPEC] + [VMEM_SPEC] * 9,
        out_specs=[VMEM_SPEC] * 2,
        scratch_shapes=[pltpu.VMEM((PACK, LANES), BF16)] + solve_scratch(),
        compiler_params=PARAMS,
        name="solve_pairs",
    )(
        total,
        pad(band),
        pad(order // slots),
        pad(weights[order]),
        bands,
        own,
        swap(own, "col", col_total, 1),
        *map(jnp.asarray, solve_tables()),
    )
    return finish(fields[0], swap(fields[1], "col", col_total, 1))


def solution(mesh):
    row_total, col_total = mesh.shape["row"], mesh.shape["col"]
    near = 2 * col_total <= 8 and row_total <= 8 and row_total * row_total * col_total <= 2 * LANES
    shards = near_shards if near else far_shards
    return jax.shard_map(
        functools.partial(shards, row_total, col_total),
        mesh=mesh,
        in_specs=(P(("row", "col"), None), P(("row", "col"), None, None), P(("row", "col"))),
        out_specs=P(("row", "col"), None),
        check_vma=False,
    )
```

time: 605 us -> 64.7 us (0.11)
  matrix products: 179 us -> 0 us
  local copies, waits for them, and re-layouts: 147 us -> 4.4 us
  waiting for transfers between devices: 133 us -> 14.1 us
  blocking collectives: 56.1 us -> 0 us
  other arithmetic: 38.3 us -> 1.66 us
  loops' own time: 35 us -> 0 us
  starting transfers between devices: 0.04 us -> 23.6 us
  Pallas kernels: 0 us -> 18.9 us
  between operations: 13.4 us -> 0.81 us
    dot_general x162 -> x0, matrix products: 179 us -> none  [the longest x160 173 us: contract(): jnp.einsum(pattern, operator, values, precision=lax.Precision.HIGHEST, pr...]
    unnamed x4 -> x0, waiting for transfers between devices: 133 us -> none
    dynamic_update_slice x16 -> x0, local copies, waits for them, and re-layouts: 95.5 us -> none  [set_row(): lax.dynamic_update_index_in_dim(terms_block, values[None, :], slot, 0)]
    all_gather x2 -> x0, blocking collectives: 56.1 us -> none  [the longest x1 46.2 us: shards(): column_block = lax.all_gather(orbitals, 'row', axis=0, tiled=True)]
    another operation x1 -> x0, loops' own time: 35 us -> none  [shards(): lax.fori_loop(0, pair_total, visit_pair, (empty_terms, empty_terms))]
    mul x17 -> x0, other arithmetic: 34.1 us -> none  [the longest x8 17.7 us: pair_terms(): distinct[pair_slot] * potential * first_wave]
    ppermute x0 -> x19, starting transfers between devices: none -> 23.6 us  [swap(): return lax.ppermute(values, axis, [(i, i ^ flip) for i in range(size)])]
    pallas_call x0 -> x3, Pallas kernels: none -> 18.9 us  [the longest x1 17.1 us: near_shards(): pl.pallas_call(functools.partial(near_kernel, row_total, col_total), out_...]
  transfers between devices with their start and end apart: 2 -> 19, of which waited for: 2 -> 7; matrix products, arithmetic and copies ran while one was open for 1% -> 5% of each run, Pallas kernels for 0% -> 0%
where the time goes in v1:
time: 64.7 us; the launch traced here: 63.5 us
  starting transfers between devices  23.6 us (36%)
  Pallas kernels  18.9 us (29%)
  waiting for transfers between devices  14.1 us (22%)
  local copies, waits for them, and re-layouts  4.4 us (7%)
  other arithmetic  1.66 us (3%)
  between operations  0.81 us (1%)
    ppermute x19, starting transfers between devices, swap(): return lax.ppermute(values, axis, [(i, i ^ flip) for i in range(size)])  23.6 us
    pallas_call x1, Pallas kernels, near_shards(): pl.pallas_call(functools.partial(near_kernel, row_total, col_total), out_...  17.1 us
    ppermute x19, waiting for transfers between devices, swap(): return lax.ppermute(values, axis, [(i, i ^ flip) for i in range(size)])  14.1 us
    unnamed x17, local copies, waits for them, and re-layouts  2.36 us
    pallas_call x1, Pallas kernels, pack_band(): pl.pallas_call(functools.partial(pack_kernel, col_total), out_shape=jax.S...  1.66 us
    unnamed x1, other arithmetic  1.66 us
    reshape x1, local copies, waits for them, and re-layouts, finish(): return field.reshape(1, LIVE * GX)  1.43 us
  transfers between devices with their start and end apart: 19, of which 7 were waited for; matrix products, arithmetic and copies ran while one was open for 5% of the time, Pallas kernels for 0%

profile of v1, /device:TPU:0, one launch (start us, length us, event | category | flops | bytes accessed | tf_op | source)
XLA Modules:
  0.0 63.5 jit_solution(2043770570445539625)
XLA Ops:
  0.0 0.5 collective-permute-start.1
  0.5 0.8 %copy.15.rest_0_ = s32[1,8,2]{2,1,0:T(8,128)S(1)} copy(s32[1,8,2]{1,2,0:T(2,128)} %param.12) | data formatting | bytes 128 | tf_op args[1]
  2.0 1.7 %reduce = bf16[64000]{0:T(1024)(128)(2,1)S(1)} reduce(bf16[1,64000]{1,0:T(2,128)(2,1)} %param.11, bf16[]{:T(256)} %constant.27), dimensions={0}, to_apply=%param.11.reduce_sub_computation | reduce | bytes 256002 | tf_op args[0]
  3.7 0.6 reshape.6.band_ref
  4.4 0.8 %copy-done.7 = bf16[3,40,128]{2,1,0:T(8,128)(2,1)S(1)} copy-done((bf16[3,40,128]{2,1,0:T(8,128)(2,1)S(1)}, bf16[3,40,128]{2,1,0:T(8,128)(2,1)}, u32[]{:S(2)}) %copy-start.7) | copy-done | bytes 30744
  5.2 1.7 %pack_band.1.refs_0_ = bf16[560,128]{1,0:T(8,128)(2,1)S(1)} custom-call(bf16[1600,40]{1,0:T(8,128)(2,1)S(1)} %reshape.6.band_ref, bf16[3,40,128]{2,1,0:T(8,128)(2,1)S(1)} %copy-done.7, s32[1,8,2]{2,1,0:T(8,128)S(1)} %copy.15.rest_0_, s32[1]{0:T(128)S(6)} %copy.16.rest_1_, s32[1,8,2]{2,1,0:T(8,128)S(1)} %collective-permute-done.rest_2_, ...), custom_call_target="tpu_custom_call" | custom-call | tf_op jit(solution)/shard_map/pack_band/pallas_call | solution.py:383
  6.8 0.5 collective-permute-start.17
  7.3 4.7 %collective-permute-start.13 = (bf16[560,128]{1,0:T(8,128)(2,1)S(1)}, bf16[560,128]{1,0:T(8,128)(2,1)S(1)}, u32[]{:S(2)}, u32[]{:S(2)}) collective-permute-start(bf16[560,128]{1,0:T(8,128)(2,1)S(1)} %pack_band.1.refs_0_), channel_id=1, source_target_pairs={{0,24},{4,28},{8,16},{12,20},{16,8},{20,12},{24,0},{28,4},{1,25},{... | collective-permute-start | bytes 430088 | tf_op jit(solution)/shard_map/ppermute | solution.py:371
  12.0 0.6 collective-permute-start.5
  12.6 1.7 %collective-permute-start.3 = (bf16[560,128]{1,0:T(8,128)(2,1)S(1)}, bf16[560,128]{1,0:T(8,128)(2,1)S(1)}, u32[]{:S(2)}, u32[]{:S(2)}) collective-permute-start(bf16[560,128]{1,0:T(8,128)(2,1)S(1)} %pack_band.1.refs_0_), channel_id=1, source_target_pairs={{0,4},{4,0},{8,12},{12,8},{16,20},{20,16},{24,28},{28,24},{1,5},{5... | collective-permute-start | bytes 430088 | tf_op jit(solution)/shard_map/ppermute | solution.py:371
  14.3 1.5 %collective-permute-start.2 = (bf16[560,128]{1,0:T(8,128)(2,1)S(1)}, bf16[560,128]{1,0:T(8,128)(2,1)S(1)}, u32[]{:S(2)}, u32[]{:S(2)}) collective-permute-start(bf16[560,128]{1,0:T(8,128)(2,1)S(1)} %pack_band.1.refs_0_), channel_id=1, source_target_pairs={{0,2},{1,3},{2,0},{3,1},{4,6},{5,7},{6,4},{7,5},{8,10},{9,11},{10,... | collective-permute-start | bytes 430088 | tf_op jit(solution)/shard_map/ppermute | solution.py:371
  15.8 0.9 %collective-permute-done.13.refs_12_ = bf16[560,128]{1,0:T(8,128)(2,1)S(1)} collective-permute-done((bf16[560,128]{1,0:T(8,128)(2,1)S(1)}, bf16[560,128]{1,0:T(8,128)(2,1)S(1)}, u32[]{:S(2)}, u32[]{:S(2)}) %collective-permute-start.13) | collective-permute-done | bytes 143392 | tf_op jit(solution)/shard_map/ppermute | solution.py:371
  16.7 1.7 %collective-permute-start.15 = (bf16[560,128]{1,0:T(8,128)(2,1)S(1)}, bf16[560,128]{1,0:T(8,128)(2,1)S(1)}, u32[]{:S(2)}, u32[]{:S(2)}) collective-permute-start(bf16[560,128]{1,0:T(8,128)(2,1)S(1)} %collective-permute-done.13.refs_12_), channel_id=1, source_target_pairs={{0,4},{4,0},{8,12},{12,8},{16,20},{20,16},{24,28},{28,24},{1,5},{5... | collective-permute-start | bytes 430088 | tf_op jit(solution)/shard_map/ppermute | solution.py:371
  18.3 6.4 %collective-permute-done.9.refs_8_ = bf16[560,128]{1,0:T(8,128)(2,1)S(1)} collective-permute-done((bf16[560,128]{1,0:T(8,128)(2,1)S(1)}, bf16[560,128]{1,0:T(8,128)(2,1)S(1)}, u32[]{:S(2)}, u32[]{:S(2)}) %collective-permute-start.9) | collective-permute-done | bytes 143392 | tf_op jit(solution)/shard_map/ppermute | solution.py:371
  24.7 1.5 %collective-permute-start.14 = (bf16[560,128]{1,0:T(8,128)(2,1)S(1)}, bf16[560,128]{1,0:T(8,128)(2,1)S(1)}, u32[]{:S(2)}, u32[]{:S(2)}) collective-permute-start(bf16[560,128]{1,0:T(8,128)(2,1)S(1)} %collective-permute-done.13.refs_12_), channel_id=1, source_target_pairs={{0,2},{1,3},{2,0},{3,1},{4,6},{5,7},{6,4},{7,5},{8,10},{9,11},{10,... | collective-permute-start | bytes 430088 | tf_op jit(solution)/shard_map/ppermute | solution.py:371
  26.2 1.5 %collective-permute-start.11 = (bf16[560,128]{1,0:T(8,128)(2,1)S(1)}, bf16[560,128]{1,0:T(8,128)(2,1)S(1)}, u32[]{:S(2)}, u32[]{:S(2)}) collective-permute-start(bf16[560,128]{1,0:T(8,128)(2,1)S(1)} %collective-permute-done.9.refs_8_), channel_id=1, source_target_pairs={{0,4},{4,0},{8,12},{12,8},{16,20},{20,16},{24,28},{28,24},{1,5},{5... | collective-permute-start | bytes 430088 | tf_op jit(solution)/shard_map/ppermute | solution.py:371
  27.7 0.5 collective-permute-start.10
  28.3 0.5 collective-permute-start.7
  28.8 1.5 %collective-permute-start.6 = (bf16[560,128]{1,0:T(8,128)(2,1)S(1)}, bf16[560,128]{1,0:T(8,128)(2,1)S(1)}, u32[]{:S(2)}, u32[]{:S(2)}) collective-permute-start(bf16[560,128]{1,0:T(8,128)(2,1)S(1)} %collective-permute-done.5.refs_4_), channel_id=1, source_target_pairs={{0,2},{1,3},{2,0},{3,1},{4,6},{5,7},{6,4},{7,5},{8,10},{9,11},{10,... | collective-permute-start | bytes 430088 | tf_op jit(solution)/shard_map/ppermute | solution.py:371
  30.3 0.4 collective-permute-done.14.refs_13_
  30.6 2.3 %collective-permute-start.4 = (bf16[560,128]{1,0:T(8,128)(2,1)S(1)}, bf16[560,128]{1,0:T(8,128)(2,1)S(1)}, u32[]{:S(2)}, u32[]{:S(2)}) collective-permute-start(bf16[560,128]{1,0:T(8,128)(2,1)S(1)} %collective-permute-done.2.refs_1_), channel_id=1, source_target_pairs={{0,4},{4,0},{8,12},{12,8},{16,20},{20,16},{24,28},{28,24},{1,5},{5... | collective-permute-start | bytes 430088 | tf_op jit(solution)/shard_map/ppermute | solution.py:371
  32.9 1.5 %collective-permute-start.16 = (bf16[560,128]{1,0:T(8,128)(2,1)S(1)}, bf16[560,128]{1,0:T(8,128)(2,1)S(1)}, u32[]{:S(2)}, u32[]{:S(2)}) collective-permute-start(bf16[560,128]{1,0:T(8,128)(2,1)S(1)} %collective-permute-done.15.refs_14_), channel_id=1, source_target_pairs={{0,2},{1,3},{2,0},{3,1},{4,6},{5,7},{6,4},{7,5},{8,10},{9,11},{10,... | collective-permute-start | bytes 430088 | tf_op jit(solution)/shard_map/ppermute | solution.py:371
  34.4 1.5 %collective-permute-start.12 = (bf16[560,128]{1,0:T(8,128)(2,1)S(1)}, bf16[560,128]{1,0:T(8,128)(2,1)S(1)}, u32[]{:S(2)}, u32[]{:S(2)}) collective-permute-start(bf16[560,128]{1,0:T(8,128)(2,1)S(1)} %collective-permute-done.10.refs_9_), channel_id=1, source_target_pairs={{0,4},{4,0},{8,12},{12,8},{16,20},{20,16},{24,28},{28,24},{1,5},{5... | collective-permute-start | bytes 430088 | tf_op jit(solution)/shard_map/ppermute | solution.py:371
  36.0 1.5 %collective-permute-start.8 = (bf16[560,128]{1,0:T(8,128)(2,1)S(1)}, bf16[560,128]{1,0:T(8,128)(2,1)S(1)}, u32[]{:S(2)}, u32[]{:S(2)}) collective-permute-start(bf16[560,128]{1,0:T(8,128)(2,1)S(1)} %collective-permute-done.7.refs_6_), channel_id=1, source_target_pairs={{0,2},{1,3},{2,0},{3,1},{4,6},{5,7},{6,4},{7,5},{8,10},{9,11},{10,... | collective-permute-start | bytes 430088 | tf_op jit(solution)/shard_map/ppermute | solution.py:371
  37.5 1.4 %collective-permute-done.4.refs_3_ = bf16[560,128]{1,0:T(8,128)(2,1)S(1)} collective-permute-done((bf16[560,128]{1,0:T(8,128)(2,1)S(1)}, bf16[560,128]{1,0:T(8,128)(2,1)S(1)}, u32[]{:S(2)}, u32[]{:S(2)}) %collective-permute-start.4) | collective-permute-done | bytes 143392 | tf_op jit(solution)/shard_map/ppermute | solution.py:371
  38.9 1.6 %collective-permute-done.16.refs_15_ = bf16[560,128]{1,0:T(8,128)(2,1)S(1)} collective-permute-done((bf16[560,128]{1,0:T(8,128)(2,1)S(1)}, bf16[560,128]{1,0:T(8,128)(2,1)S(1)}, u32[]{:S(2)}, u32[]{:S(2)}) %collective-permute-start.16) | collective-permute-done | bytes 143392 | tf_op jit(solution)/shard_map/ppermute | solution.py:371
  40.6 1.7 %collective-permute-done.8.refs_7_ = bf16[560,128]{1,0:T(8,128)(2,1)S(1)} collective-permute-done((bf16[560,128]{1,0:T(8,128)(2,1)S(1)}, bf16[560,128]{1,0:T(8,128)(2,1)S(1)}, u32[]{:S(2)}, u32[]{:S(2)}) %collective-permute-start.8) | collective-permute-done | bytes 143392 | tf_op jit(solution)/shard_map/ppermute | solution.py:371
  42.4 0.8 %copy-done.6 = bf16[80,240]{1,0:T(8,128)(2,1)S(1)} copy-done((bf16[80,240]{1,0:T(8,128)(2,1)S(1)}, bf16[80,240]{1,0:T(8,128)(2,1)}, u32[]{:S(2)}) %copy-start.6) | copy-done | bytes 38424
  43.1 17.1 %solve_pairs.1 = (f32[560,128]{1,0:T(8,128)S(1)}, f32[560,128]{1,0:T(8,128)S(1)}) custom-call(bf16[560,128]{1,0:T(8,128)(2,1)S(1)} %pack_band.1.refs_0_, bf16[560,128]{1,0:T(8,128)(2,1)S(1)} %collective-permute-done.2.refs_1_, bf16[560,128]{1,0:T(8,128)(2,1)S(1)} %collective-permute-done.3.refs_2_, bf16[560,128]{1,0:T(8,128)(2,1)S(1)} %collective-permute-done.4.refs_3_, ...), custom_call_target="tpu_custom_call" | custom-call | tf_op jit(solution)/shard_map/solve_pairs/pallas_call | solution.py:430
  60.3 1.6 %collective-permute-done.18.part_ref = f32[560,128]{1,0:T(8,128)S(1)} collective-permute-done((f32[560,128]{1,0:T(8,128)S(1)}, f32[560,128]{1,0:T(8,128)S(1)}, u32[]{:S(2)}, u32[]{:S(2)}) %collective-permute-start.18) | collective-permute-done | bytes 286752 | tf_op jit(solution)/shard_map/ppermute | solution.py:371
  61.8 0.2 add_parts.1
  62.0 1.4 %reshape.7 = f32[1,64000]{1,0:T(1,128)} reshape(f32[1600,40]{1,0:T(8,128)S(1)} %add_parts.1) | data formatting | bytes 512000 | tf_op jit(solution)/shard_map/reshape | solution.py:402
  (29 shorter events, 0.3 us)
Async XLA Ops:
  0.0 42.3 %copy-start = (f32[1600,128]{1,0:T(8,128)S(1)}, f32[1600,128]{1,0:T(8,128)}, u32[]{:S(2)}) copy-start(f32[1600,128]{1,0:T(8,128)} %constant.23.clone.refs_23_) | copy-start | bytes 2457604
  0.0 4.3 %collective-permute-start.1 = (s32[1]{0:T(128)}, s32[1]{0:T(128)}, u32[]{:S(2)}, u32[]{:S(2)}) collective-permute-start(s32[1]{0:T(128)} %param.13), channel_id=1, source_target_pairs={{0,1},{1,0},{2,3},{3,2},{4,5},{5,4},{6,7},{7,6},{8,9},{9,8},{10,11... | collective-permute-start | bytes 20 | tf_op jit(solution)/shard_map/ppermute | solution.py:371
  1.2 3.1 %collective-permute-start = (s32[1,8,2]{2,1,0:T(8,128)S(1)}, s32[1,8,2]{2,1,0:T(8,128)S(1)}, u32[]{:S(2)}, u32[]{:S(2)}) collective-permute-start(s32[1,8,2]{2,1,0:T(8,128)S(1)} %copy.15.rest_0_), channel_id=1, source_target_pairs={{0,1},{1,0},{2,3},{3,2},{4,5},{5,4},{6,7},{7,6},{8,9},{9,8},{10,11... | collective-permute-start | bytes 200 | tf_op jit(solution)/shard_map/ppermute | solution.py:371
  3.6 38.7 %copy-start.4 = (bf16[128,384]{1,0:T(8,128)(2,1)S(1)}, bf16[128,384]{1,0:T(8,128)(2,1)}, u32[]{:S(2)}) copy-start(bf16[128,384]{1,0:T(8,128)(2,1)} %constant.18.clone.refs_18_) | copy-start | bytes 294916
  3.7 38.7 %copy-start.5 = (bf16[80,240]{1,0:T(8,128)(2,1)S(1)}, bf16[80,240]{1,0:T(8,128)(2,1)}, u32[]{:S(2)}) copy-start(bf16[80,240]{1,0:T(8,128)(2,1)} %constant.22.clone.refs_22_) | copy-start | bytes 115204
  4.3 38.0 %copy-start.1 = (bf16[384,384]{1,0:T(8,128)(2,1)S(1)}, bf16[384,384]{1,0:T(8,128)(2,1)}, u32[]{:S(2)}) copy-start(bf16[384,384]{1,0:T(8,128)(2,1)} %constant.17.clone.refs_17_) | copy-start | bytes 884740
  4.3 38.0 %copy-start.2 = (bf16[256,256]{1,0:T(8,128)(2,1)S(1)}, bf16[256,256]{1,0:T(8,128)(2,1)}, u32[]{:S(2)}) copy-start(bf16[256,256]{1,0:T(8,128)(2,1)} %constant.20.clone.refs_20_) | copy-start | bytes 393220
  4.3 38.0 %copy-start.3 = (bf16[256,256]{1,0:T(8,128)(2,1)S(1)}, bf16[256,256]{1,0:T(8,128)(2,1)}, u32[]{:S(2)}) copy-start(bf16[256,256]{1,0:T(8,128)(2,1)} %constant.19.clone.refs_19_) | copy-start | bytes 393220
  4.3 0.8 %copy-start.7 = (bf16[3,40,128]{2,1,0:T(8,128)(2,1)S(1)}, bf16[3,40,128]{2,1,0:T(8,128)(2,1)}, u32[]{:S(2)}) copy-start(bf16[3,40,128]{2,1,0:T(8,128)(2,1)} %constant.16.clone.table_ref) | copy-start | bytes 92164
  6.8 7.4 %collective-permute-start.17 = (bf16[560,128]{1,0:T(8,128)(2,1)S(1)}, bf16[560,128]{1,0:T(8,128)(2,1)S(1)}, u32[]{:S(2)}, u32[]{:S(2)}) collective-permute-start(bf16[560,128]{1,0:T(8,128)(2,1)S(1)} %pack_band.1.refs_0_), channel_id=1, source_target_pairs={{0,1},{1,0},{2,3},{3,2},{4,5},{5,4},{6,7},{7,6},{8,9},{9,8},{10,11... | collective-permute-start | bytes 430088 | tf_op jit(solution)/shard_map/ppermute | solution.py:371
  7.3 9.4 %collective-permute-start.13 = (bf16[560,128]{1,0:T(8,128)(2,1)S(1)}, bf16[560,128]{1,0:T(8,128)(2,1)S(1)}, u32[]{:S(2)}, u32[]{:S(2)}) collective-permute-start(bf16[560,128]{1,0:T(8,128)(2,1)S(1)} %pack_band.1.refs_0_), channel_id=1, source_target_pairs={{0,24},{4,28},{8,16},{12,20},{16,8},{20,12},{24,0},{28,4},{1,25},{... | collective-permute-start | bytes 430088 | tf_op jit(solution)/shard_map/ppermute | solution.py:371
  12.0 12.7 %collective-permute-start.9 = (bf16[560,128]{1,0:T(8,128)(2,1)S(1)}, bf16[560,128]{1,0:T(8,128)(2,1)S(1)}, u32[]{:S(2)}, u32[]{:S(2)}) collective-permute-start(bf16[560,128]{1,0:T(8,128)(2,1)S(1)} %pack_band.1.refs_0_), channel_id=1, source_target_pairs={{0,16},{4,20},{8,24},{12,28},{16,0},{20,4},{24,8},{28,12},{1,17},{... | collective-permute-start | bytes 430088 | tf_op jit(solution)/shard_map/ppermute | solution.py:371
  12.0 14.2 %collective-permute-start.5 = (bf16[560,128]{1,0:T(8,128)(2,1)S(1)}, bf16[560,128]{1,0:T(8,128)(2,1)S(1)}, u32[]{:S(2)}, u32[]{:S(2)}) collective-permute-start(bf16[560,128]{1,0:T(8,128)(2,1)S(1)} %pack_band.1.refs_0_), channel_id=1, source_target_pairs={{0,8},{4,12},{8,0},{12,4},{16,24},{20,28},{24,16},{28,20},{1,9},{5... | collective-permute-start | bytes 430088 | tf_op jit(solution)/shard_map/ppermute | solution.py:371
  12.6 15.1 %collective-permute-start.3 = (bf16[560,128]{1,0:T(8,128)(2,1)S(1)}, bf16[560,128]{1,0:T(8,128)(2,1)S(1)}, u32[]{:S(2)}, u32[]{:S(2)}) collective-permute-start(bf16[560,128]{1,0:T(8,128)(2,1)S(1)} %pack_band.1.refs_0_), channel_id=1, source_target_pairs={{0,4},{4,0},{8,12},{12,8},{16,20},{20,16},{24,28},{28,24},{1,5},{5... | collective-permute-start | bytes 430088 | tf_op jit(solution)/shard_map/ppermute | solution.py:371
  14.3 14.0 %collective-permute-start.2 = (bf16[560,128]{1,0:T(8,128)(2,1)S(1)}, bf16[560,128]{1,0:T(8,128)(2,1)S(1)}, u32[]{:S(2)}, u32[]{:S(2)}) collective-permute-start(bf16[560,128]{1,0:T(8,128)(2,1)S(1)} %pack_band.1.refs_0_), channel_id=1, source_target_pairs={{0,2},{1,3},{2,0},{3,1},{4,6},{5,7},{6,4},{7,5},{8,10},{9,11},{10,... | collective-permute-start | bytes 430088 | tf_op jit(solution)/shard_map/ppermute | solution.py:371
  16.7 12.1 %collective-permute-start.15 = (bf16[560,128]{1,0:T(8,128)(2,1)S(1)}, bf16[560,128]{1,0:T(8,128)(2,1)S(1)}, u32[]{:S(2)}, u32[]{:S(2)}) collective-permute-start(bf16[560,128]{1,0:T(8,128)(2,1)S(1)} %collective-permute-done.13.refs_12_), channel_id=1, source_target_pairs={{0,4},{4,0},{8,12},{12,8},{16,20},{20,16},{24,28},{28,24},{1,5},{5... | collective-permute-start | bytes 430088 | tf_op jit(solution)/shard_map/ppermute | solution.py:371
  24.7 5.9 %collective-permute-start.14 = (bf16[560,128]{1,0:T(8,128)(2,1)S(1)}, bf16[560,128]{1,0:T(8,128)(2,1)S(1)}, u32[]{:S(2)}, u32[]{:S(2)}) collective-permute-start(bf16[560,128]{1,0:T(8,128)(2,1)S(1)} %collective-permute-done.13.refs_12_), channel_id=1, source_target_pairs={{0,2},{1,3},{2,0},{3,1},{4,6},{5,7},{6,4},{7,5},{8,10},{9,11},{10,... | collective-permute-start | bytes 430088 | tf_op jit(solution)/shard_map/ppermute | solution.py:371
  26.2 6.7 %collective-permute-start.11 = (bf16[560,128]{1,0:T(8,128)(2,1)S(1)}, bf16[560,128]{1,0:T(8,128)(2,1)S(1)}, u32[]{:S(2)}, u32[]{:S(2)}) collective-permute-start(bf16[560,128]{1,0:T(8,128)(2,1)S(1)} %collective-permute-done.9.refs_8_), channel_id=1, source_target_pairs={{0,4},{4,0},{8,12},{12,8},{16,20},{20,16},{24,28},{28,24},{1,5},{5... | collective-permute-start | bytes 430088 | tf_op jit(solution)/shard_map/ppermute | solution.py:371
  27.7 6.7 %collective-permute-start.10 = (bf16[560,128]{1,0:T(8,128)(2,1)S(1)}, bf16[560,128]{1,0:T(8,128)(2,1)S(1)}, u32[]{:S(2)}, u32[]{:S(2)}) collective-permute-start(bf16[560,128]{1,0:T(8,128)(2,1)S(1)} %collective-permute-done.9.refs_8_), channel_id=1, source_target_pairs={{0,2},{1,3},{2,0},{3,1},{4,6},{5,7},{6,4},{7,5},{8,10},{9,11},{10,... | collective-permute-start | bytes 430088 | tf_op jit(solution)/shard_map/ppermute | solution.py:371
  28.3 7.7 %collective-permute-start.7 = (bf16[560,128]{1,0:T(8,128)(2,1)S(1)}, bf16[560,128]{1,0:T(8,128)(2,1)S(1)}, u32[]{:S(2)}, u32[]{:S(2)}) collective-permute-start(bf16[560,128]{1,0:T(8,128)(2,1)S(1)} %collective-permute-done.5.refs_4_), channel_id=1, source_target_pairs={{0,4},{4,0},{8,12},{12,8},{16,20},{20,16},{24,28},{28,24},{1,5},{5... | collective-permute-start | bytes 430088 | tf_op jit(solution)/shard_map/ppermute | solution.py:371
  28.8 8.7 %collective-permute-start.6 = (bf16[560,128]{1,0:T(8,128)(2,1)S(1)}, bf16[560,128]{1,0:T(8,128)(2,1)S(1)}, u32[]{:S(2)}, u32[]{:S(2)}) collective-permute-start(bf16[560,128]{1,0:T(8,128)(2,1)S(1)} %collective-permute-done.5.refs_4_), channel_id=1, source_target_pairs={{0,2},{1,3},{2,0},{3,1},{4,6},{5,7},{6,4},{7,5},{8,10},{9,11},{10,... | collective-permute-start | bytes 430088 | tf_op jit(solution)/shard_map/ppermute | solution.py:371
  30.6 8.3 %collective-permute-start.4 = (bf16[560,128]{1,0:T(8,128)(2,1)S(1)}, bf16[560,128]{1,0:T(8,128)(2,1)S(1)}, u32[]{:S(2)}, u32[]{:S(2)}) collective-permute-start(bf16[560,128]{1,0:T(8,128)(2,1)S(1)} %collective-permute-done.2.refs_1_), channel_id=1, source_target_pairs={{0,4},{4,0},{8,12},{12,8},{16,20},{20,16},{24,28},{28,24},{1,5},{5... | collective-permute-start | bytes 430088 | tf_op jit(solution)/shard_map/ppermute | solution.py:371
  32.9 7.7 %collective-permute-start.16 = (bf16[560,128]{1,0:T(8,128)(2,1)S(1)}, bf16[560,128]{1,0:T(8,128)(2,1)S(1)}, u32[]{:S(2)}, u32[]{:S(2)}) collective-permute-start(bf16[560,128]{1,0:T(8,128)(2,1)S(1)} %collective-permute-done.15.refs_14_), channel_id=1, source_target_pairs={{0,2},{1,3},{2,0},{3,1},{4,6},{5,7},{6,4},{7,5},{8,10},{9,11},{10,... | collective-permute-start | bytes 430088 | tf_op jit(solution)/shard_map/ppermute | solution.py:371
  34.4 6.1 %collective-permute-start.12 = (bf16[560,128]{1,0:T(8,128)(2,1)S(1)}, bf16[560,128]{1,0:T(8,128)(2,1)S(1)}, u32[]{:S(2)}, u32[]{:S(2)}) collective-permute-start(bf16[560,128]{1,0:T(8,128)(2,1)S(1)} %collective-permute-done.10.refs_9_), channel_id=1, source_target_pairs={{0,4},{4,0},{8,12},{12,8},{16,20},{20,16},{24,28},{28,24},{1,5},{5... | collective-permute-start | bytes 430088 | tf_op jit(solution)/shard_map/ppermute | solution.py:371
  36.0 6.3 %collective-permute-start.8 = (bf16[560,128]{1,0:T(8,128)(2,1)S(1)}, bf16[560,128]{1,0:T(8,128)(2,1)S(1)}, u32[]{:S(2)}, u32[]{:S(2)}) collective-permute-start(bf16[560,128]{1,0:T(8,128)(2,1)S(1)} %collective-permute-done.7.refs_6_), channel_id=1, source_target_pairs={{0,2},{1,3},{2,0},{3,1},{4,6},{5,7},{6,4},{7,5},{8,10},{9,11},{10,... | collective-permute-start | bytes 430088 | tf_op jit(solution)/shard_map/ppermute | solution.py:371
  42.3 0.8 %copy-start.6 = (bf16[80,240]{1,0:T(8,128)(2,1)S(1)}, bf16[80,240]{1,0:T(8,128)(2,1)}, u32[]{:S(2)}) copy-start(bf16[80,240]{1,0:T(8,128)(2,1)} %constant.21.clone.refs_21_) | copy-start | bytes 115204
  60.2 1.6 %collective-permute-start.18 = (f32[560,128]{1,0:T(8,128)S(1)}, f32[560,128]{1,0:T(8,128)S(1)}, u32[]{:S(2)}, u32[]{:S(2)}) collective-permute-start(f32[560,128]{1,0:T(8,128)S(1)} %get-tuple-element.8), channel_id=1, source_target_pairs={{0,1},{1,0},{2,3},{3,2},{4,5},{5,4},{6,7},{7,6},{8,9},{9,8},{10,11... | collective-permute-start | bytes 860168 | tf_op jit(solution)/shard_map/ppermute | solution.py:371

commit v2 on v1

--- a/solution.py
+++ b/solution.py
@@ -1,4 +1,5 @@
 import functools
+import itertools
 
 import jax
 import jax.numpy as jnp
@@ -19,8 +20,8 @@
 SPARE = SIDE * GX
 DUO = 2 * GX
 QUAD = 4 * GX
-GROUP = 5
-VMEM_LIMIT = 48 * 1024 * 1024
+GROUP = 10
+VMEM_LIMIT = 20 * 1024 * 1024
 screen_width = 0.9
 F32 = jnp.float32
 BF16 = jnp.bfloat16
@@ -151,15 +152,14 @@
         ref[pl.ds(step * 4 + i, GX, stride=GX), :] = values[rows : rows + GX, lanes : lanes + LANES]
 
 
-def count_vector(list_ref, count_ref, first_row):
-    row = lax.broadcasted_iota(jnp.int32, (8, LANES), 0) - first_row
-    lane = lax.broadcasted_iota(jnp.int32, (8, LANES), 1) - SPARE
-    counts = jnp.zeros((8, LANES), F32)
-    for p in range(list_ref.shape[1]):
-        here = (row == list_ref[0, p, 0]) & (lane == list_ref[0, p, 1])
-        live = jnp.where(p < count_ref[0], 1.0, 0.0)
-        counts = counts + jnp.where(here, live, 0.0)
-    return counts
+def count_vector(list_ref, first_row):
+    pairs = list_ref[0]
+    slots = pairs.shape[0]
+    row = lax.broadcasted_iota(jnp.int32, (slots, LANES), 1) - first_row
+    lane = lax.broadcasted_iota(jnp.int32, (slots, LANES), 1) - SPARE
+    first = jnp.where(pairs[:, 0:1] == row, 1.0, 0.0)
+    second = jnp.where(pairs[:, 1:2] == lane, 1.0, 0.0)
+    return lax.dot_general(first, second, (((0,), (0,)), ((), ())), preferred_element_type=F32)
 
 
 def pack_kernel(col_total, band_ref, table_ref, *rest):
@@ -172,10 +172,11 @@
             piece = jnp.concatenate([piece, jnp.zeros((PACK - rows, LANES), F32)], axis=0)
         total = piece if total is None else total + piece
     if len(rest) > 1:
-        counts = count_vector(rest[0], rest[1], 0) + count_vector(rest[2], rest[3], col_total)
+        counts = sum(count_vector(ref, k * col_total) for k, ref in enumerate(rest[:-1]))
+        counts = counts[:16]
         empty = jnp.zeros((PACK - counts.shape[0], LANES), F32)
         total = total + jnp.concatenate([counts, empty], axis=0)
-    out_ref[...] = total.astype(BF16)
+    out_ref[0] = total.astype(BF16)
 
 
 def spread_waves(own_bands, repeat_ref, wave_refs):
@@ -185,14 +186,20 @@
             wave_ref[pl.ds(third * PACK, PACK), :] = wide[:, third * LANES : (third + 1) * LANES]
 
 
-def solve_pairs(total, lists, load_band, tables, out_refs, scratch):
-    spread_ref, repeat_ref, z_ref, z_back_ref, row_ref, row_back_ref, kernel_ref = tables
-    trio_ref, *wave_refs, partner_ref, work_ref, work2_ref, sum0_ref, sum1_ref = scratch
-    sum_refs = (sum0_ref, sum1_ref)
-    slot_list, band_list, weight_list = lists
+def clear(sum_refs):
     for sum_ref in sum_refs:
         sum_ref[...] = jnp.zeros_like(sum_ref)
-    side = lax.broadcasted_iota(jnp.int32, (1, LANES), 1) // GX
+
+
+def lane_side():
+    return lax.broadcasted_iota(jnp.int32, (1, LANES), 1) // GX
+
+
+def solve_trios(first, count, lists, load_band, tables, wave_refs, sum_refs, scratch):
+    spread_ref, _, z_ref, z_back_ref, row_ref, row_back_ref, kernel_ref = tables
+    trio_ref, partner_ref, work_ref, work2_ref = scratch
+    slot_list, band_list, weight_list = lists
+    side = lane_side()
 
     def by_side(values):
         row = jnp.zeros((1, LANES), F32)
@@ -201,7 +208,7 @@
         return row
 
     def trio(at, carry):
-        places = [at * SIDE + p for p in range(SIDE)]
+        places = [first + at * SIDE + p for p in range(SIDE)]
         for p, place in enumerate(places):
             load_band(slot_list[place], trio_ref, p)
         bands = [band_list[place] for place in places]
@@ -246,7 +253,11 @@
             in_groups(phase)
         return carry
 
-    lax.fori_loop(0, (total + SIDE - 1) // SIDE, trio, 0)
+    lax.fori_loop(0, count, trio, 0)
+
+
+def pack_fields(sum_refs, out_refs):
+    side = lane_side()
 
     def pack_sums(step, carry):
         for out_ref, sum_ref in zip(out_refs, sum_refs):
@@ -264,70 +275,96 @@
     lax.fori_loop(0, THIRD, pack_sums, 0)
 
 
-def near_kernel(row_total, col_total, *refs):
-    pairs_wide = col_total // 2
-    slots = row_total * pairs_wide
-    band_refs, refs = refs[:slots], refs[slots:]
-    mate_ref, tables, out_refs, refs = refs[0], refs[1:8], refs[8:10], refs[10:]
+def near_kernel(row_total, col_total, part, *refs):
+    stages = STAGES[: part + 1]
+    blocks = [block for stage in stages for block in stage]
+    band_refs, refs = refs[: len(blocks)], refs[len(blocks) :]
+    bands = [(ref, at) for ref, block in zip(band_refs, blocks) for at in range(len(block))]
+    flips = [flip for block in blocks for flip in block]
+    mate_ref, tables, refs = refs[0], refs[1:8], refs[8:]
+    if part:
+        wave_refs, given_refs, out_refs, refs = refs[:2], refs[2:4], refs[4:6], refs[6:]
+    else:
+        wave_refs, out_refs, refs = refs[:2], refs[2:4], refs[4:]
     (count_vmem, count_smem, slot_list, band_list, weight_list), refs = refs[:5], refs[5:]
-    scratch, sem = refs[:-1], refs[-1]
+    scratch, sem = refs[:4], refs[4]
+    sum_refs = refs[5:] if part == 2 else out_refs
 
     lane = lax.broadcasted_iota(jnp.int32, (8, LANES), 1)
     counts = jnp.zeros((8, LANES), F32)
-    for s in range(slots):
-        spare = band_refs[s][0:16, :].astype(F32)[0:8]
+    for s, (ref, at) in enumerate(bands):
+        spare = ref[at, 0:16, :].astype(F32)[0:8]
         shift = (s * row_total - SPARE) % LANES
         moved = pltpu.roll(spare, shift, 1) if shift else spare
         counts = jnp.where(lane // row_total == s, moved, counts)
     count_vmem[...] = counts.astype(jnp.int32)
     copy = pltpu.make_async_copy(count_vmem, count_smem, sem)
     copy.start()
-    spread_waves((band_refs[0][...], mate_ref[...]), tables[1], scratch[1:3])
+    if part:
+        for sum_ref, given_ref in zip(sum_refs, given_refs):
+            sum_ref[...] = given_ref[...]
+    else:
+        clear(sum_refs)
+        spread_waves((band_refs[0][0], mate_ref[0]), tables[1], wave_refs)
     copy.wait()
     row = lax.axis_index("row")
     col = lax.axis_index("col")
     total = jnp.int32(0)
-    for which in range(2):
-        mine = col ^ which
-        for slot in range(slots):
-            row_flip, x_flip = slot // pairs_wide, slot % pairs_wide
-            other_row = row ^ row_flip
-            other_col = col ^ (2 * x_flip)
-            weight = count_smem[mine, x_flip * row_total + other_row]
-            if which or slot:
-                mirror_lane = row_flip * pairs_wide * row_total + row
-                weight = weight + count_smem[which * col_total + other_col, mirror_lane]
-            slot_list[total] = slot
+    done = jnp.int32(0)
+    place = 0
+    for step, stage in enumerate(stages):
+        here = range(place, place + sum(len(block) for block in stage))
+        place = here.stop
+        for which, at in itertools.product(range(2), here):
+            row_flip, col_flip = flips[at]
+            row_place = flips.index((0, col_flip)) * row_total
+            col_place = flips.index((row_flip, 0)) * row_total
+            weight = count_smem[col ^ which, row_place + (row ^ row_flip)]
+            if at or which:
+                mirror = which * col_total + (col ^ col_flip)
+                weight = weight + count_smem[mirror, col_place + row]
+            slot_list[total] = at
             band_list[total] = which
             weight_list[total] = weight
             total = total + jnp.where(weight > 0, 1, 0)
+        if step < 2:
+            trios = jnp.minimum((total - done) // SIDE, CAPS[step])
+            if step < part:
+                done = done + trios * SIDE
+    if part == 2:
+        trios = (total - done + SIDE - 1) // SIDE
+        for p in range(SIDE - 1):
+            slot_list[total + p] = 0
+            band_list[total + p] = 0
+            weight_list[total + p] = 0
+
+    def load_band(wanted, target, p):
+        for place, (ref, at) in enumerate(bands):
+
+            @pl.when(wanted == place)
+            def _():
+                target[:, p * LANES : (p + 1) * LANES] = ref[at]
+
     lists = (slot_list, band_list, weight_list)
-    for p in range(SIDE - 1):
-        slot_list[total + p] = 0
-        band_list[total + p] = 0
-        weight_list[total + p] = 0
-
-    def load_band(place, target, p):
-        for s in range(slots):
-
-            @pl.when(place == s)
-            def _():
-                target[:, p * LANES : (p + 1) * LANES] = band_refs[s][...]
-
-    solve_pairs(total, lists, load_band, tables, out_refs, scratch)
+    solve_trios(done, trios, lists, load_band, tables, wave_refs, sum_refs, scratch)
+    if part == 2:
+        pack_fields(sum_refs, out_refs)
 
 
 def far_kernel(total_ref, slot_list, band_list, weight_list, bands_ref, own_ref, mate_ref, *refs):
     tables, out_refs, refs = refs[:7], refs[7:9], refs[9:]
-    buffer, scratch = refs[0], refs[1:]
-    spread_waves((own_ref[...], mate_ref[...]), tables[1], scratch[1:3])
+    buffer, wave_refs, sum_refs, scratch = refs[0], refs[1:3], refs[3:5], refs[5:]
+    spread_waves((own_ref[0], mate_ref[0]), tables[1], wave_refs)
+    clear(sum_refs)
 
     def load_band(place, target, p):
         pltpu.sync_copy(bands_ref.at[place], buffer)
         target[:, p * LANES : (p + 1) * LANES] = buffer[...]
 
     lists = (slot_list, band_list, weight_list)
-    solve_pairs(total_ref[0], lists, load_band, tables, out_refs, scratch)
+    trios = (total_ref[0] + SIDE - 1) // SIDE
+    solve_trios(0, trios, lists, load_band, tables, wave_refs, sum_refs, scratch)
+    pack_fields(sum_refs, out_refs)
 
 
 def finish_kernel(own_ref, part_ref, out_ref):
@@ -359,12 +396,11 @@
 
 
 def solve_scratch():
-    wide = pltpu.VMEM((ROWS, LANES), F32)
-    return [pltpu.VMEM((PACK, SIDE * LANES), BF16)] + [wide] * 7
-
-
-def field_shapes():
-    return [jax.ShapeDtypeStruct((PACK, LANES), F32)] * 2
+    return [pltpu.VMEM((PACK, SIDE * LANES), BF16)] + [pltpu.VMEM((ROWS, LANES), F32)] * 3
+
+
+def pair_of(rows):
+    return [jax.ShapeDtypeStruct((rows, LANES), F32)] * 2
 
 
 def swap(values, axis, size, flip):
@@ -382,8 +418,8 @@
 def pack_band(orbitals, col_total, extras):
     return pl.pallas_call(
         functools.partial(pack_kernel, col_total),
-        out_shape=jax.ShapeDtypeStruct((PACK, LANES), BF16),
-        in_specs=[VMEM_SPEC] * 2 + [SMEM_SPEC] * len(extras),
+        out_shape=jax.ShapeDtypeStruct((1, PACK, LANES), BF16),
+        in_specs=[VMEM_SPEC] * (2 + len(extras)),
         out_specs=VMEM_SPEC,
         compiler_params=PARAMS,
         name="pack_band",
@@ -402,36 +438,29 @@
     return field.reshape(1, LIVE * GX)
 
 
-def near_shards(row_total, col_total, orbitals, pair_list, pair_count):
-    row_swap = lambda values, flip: swap(values, "row", row_total, flip)
-    col_swap = lambda values, flip: swap(values, "col", col_total, flip)
-    extras = (pair_list, pair_count, col_swap(pair_list, 1), col_swap(pair_count, 1))
-    own = pack_band(orbitals, col_total, extras)
-    wide = col_total // 2
-    bands = {(0, 0, 0): own}
-    for z in range(1, row_total // 2):
-        bands[z, 0, 0] = row_swap(own, 2 * z)
-    for z in range(row_total // 2):
-        for x in range(1, wide):
-            bands[z, 0, x] = col_swap(bands[z, 0, 0], 2 * x)
-        bands[z, 1, 0] = row_swap(bands[z, 0, 0], 1)
-    for z in range(row_total // 2):
-        for x in range(1, wide):
-            if z % 2:
-                bands[z, 1, x] = col_swap(bands[z, 1, 0], 2 * x)
-            else:
-                bands[z, 1, x] = row_swap(bands[z, 0, x], 1)
-    mate = col_swap(own, 1)
-    slots = row_total * wide
-    ordered = [
-        bands[s // wide // 2, s // wide % 2, s % wide] for s in range(slots)
-    ]
-    places = 2 * slots + SIDE
-    fields = pl.pallas_call(
-        functools.partial(near_kernel, row_total, col_total),
-        out_shape=field_shapes(),
-        in_specs=[VMEM_SPEC] * (slots + 8),
-        out_specs=[VMEM_SPEC] * 2,
+NEAR = (8, 4)
+STAGES = (
+    (((0, 0),), ((4, 0),), ((2, 0),), ((1, 0),), ((0, 2),)),
+    (((4, 2), (2, 2)), ((5, 0), (1, 2)), ((6, 0), (3, 0))),
+    (((6, 2),), ((5, 2),), ((7, 0), (3, 2)), ((7, 2),)),
+)
+CAPS = (2, 2)
+
+
+def near_part(row_total, col_total, part, operands):
+    places = 2 * row_total * (col_total // 2) + SIDE
+    out_shape = pair_of(ROWS)
+    if part == 0:
+        out_shape = out_shape * 2
+    if part == 2:
+        out_shape = pair_of(PACK)
+    operands = list(operands)
+    cost = pl.CostEstimate(flops=4 * 10**9, bytes_accessed=2 * 10**7, transcendentals=0)
+    return pl.pallas_call(
+        functools.partial(near_kernel, row_total, col_total, part),
+        out_shape=out_shape,
+        in_specs=[VMEM_SPEC] * len(operands),
+        out_specs=[VMEM_SPEC] * len(out_shape),
         scratch_shapes=[
             pltpu.VMEM((8, LANES), jnp.int32),
             pltpu.SMEM((8, LANES), jnp.int32),
@@ -440,11 +469,39 @@
             pltpu.SMEM((places,), jnp.int32),
         ]
         + solve_scratch()
-        + [pltpu.SemaphoreType.DMA],
+        + [pltpu.SemaphoreType.DMA]
+        + [pltpu.VMEM((ROWS, LANES), F32)] * (2 if part == 2 else 0),
         compiler_params=PARAMS,
-        name="solve_pairs",
-    )(*ordered, mate, *map(jnp.asarray, solve_tables()))
-    return finish(fields[0], col_swap(fields[1], 1))
+        cost_estimate=cost,
+        name="solve_part",
+    )(*operands)
+
+
+def near_shards(row_total, col_total, orbitals, pair_list, pair_count):
+    row_swap = lambda values, flip: swap(values, "row", row_total, flip)
+    col_swap = lambda values, flip: swap(values, "col", col_total, flip)
+    both = lambda a, b: jnp.concatenate([a, b], axis=0)
+    live = lax.iota(jnp.int32, pair_list.shape[1])[None, :, None] < pair_count[0]
+    pairs = jnp.where(live, pair_list, -row_total * col_total)
+    own = pack_band(orbitals, col_total, [pairs, col_swap(pairs, 1)])
+    w, z, y, x = row_swap(own, 4), row_swap(own, 2), row_swap(own, 1), col_swap(own, 2)
+    mate = col_swap(own, 1)
+    over_x, over_y, over_z = col_swap(both(w, z), 2), row_swap(both(w, x), 1), row_swap(both(w, y), 2)
+    tables = [jnp.asarray(table) for table in solve_tables()]
+    blocks = [own, w, z, y, x]
+    *waves, sum0, sum1 = near_part(row_total, col_total, 0, [*blocks, mate, *tables])
+    held = lax.optimization_barrier((sum0, sum1, over_x, over_y, over_z))
+    sum0, sum1, over_x, over_y, over_z = held
+    wzx = col_swap(over_z[:1], 2)
+    wxy = row_swap(over_x[:1], 1)
+    wyz_xyz = row_swap(over_y, 2)
+    wzxy = row_swap(wzx, 1)
+    arrivals = ((over_x, over_y, over_z), (wzx, wxy, wyz_xyz, wzxy))
+    for part, arrived in enumerate(arrivals, 1):
+        blocks += arrived
+        operands = [*blocks, mate, *tables, *waves, sum0, sum1]
+        sum0, sum1 = near_part(row_total, col_total, part, operands)
+    return finish(sum0, col_swap(sum1, 1))
 
 
 def far_shards(row_total, col_total, orbitals, pair_list, pair_count):
@@ -454,7 +511,7 @@
     table = lax.all_gather(counts.reshape(-1), axes)
     table = table.reshape(row_total, col_total, col_total, row_total)
     wide = col_total // 2
-    column = lax.all_gather(own, "row")
+    column = lax.all_gather(own[0], "row")
     columns = [column] + [swap(column, "col", col_total, 2 * x) for x in range(1, wide)]
     bands = jnp.concatenate(columns, axis=0)
     row = lax.axis_index("row")
@@ -477,10 +534,12 @@
     total = jnp.sum((weights > 0).astype(jnp.int32)).reshape(1)
     fields = pl.pallas_call(
         far_kernel,
-        out_shape=field_shapes(),
+        out_shape=pair_of(PACK),
         in_specs=[SMEM_SPEC] * 4 + [ANY_SPEC] + [VMEM_SPEC] * 9,
         out_specs=[VMEM_SPEC] * 2,
-        scratch_shapes=[pltpu.VMEM((PACK, LANES), BF16)] + solve_scratch(),
+        scratch_shapes=[pltpu.VMEM((PACK, LANES), BF16)]
+        + [pltpu.VMEM((ROWS, LANES), F32)] * 4
+        + solve_scratch(),
         compiler_params=PARAMS,
         name="solve_pairs",
     )(
@@ -498,7 +557,7 @@
 
 def solution(mesh):
     row_total, col_total = mesh.shape["row"], mesh.shape["col"]
-    near = 2 * col_total <= 8 and row_total <= 8 and row_total * row_total * col_total <= 2 * LANES
+    near = (row_total, col_total) == NEAR
     shards = near_shards if near else far_shards
     return jax.shard_map(
         functools.partial(shards, row_total, col_total),

time: 64.7 us -> 49.7 us (0.77); the launches traced: 63.5 us -> 49.6 us
  starting transfers between devices: 23.6 us -> 15.9 us
  Pallas kernels: 18.9 us -> 12.9 us
  local copies, waits for them, and re-layouts: 4.4 us -> 2.96 us
  waiting for transfers between devices: 14.1 us -> 15.2 us
    ppermute x19 -> x14, starting transfers between devices: 23.6 us -> 15.9 us  [swap(): return lax.ppermute(values, axis, [(i, i ^ flip) for i in range(size)])]
    pallas_call x1 -> x3, Pallas kernels: 17.1 us -> 12.4 us  [near_part(): pl.pallas_call(functools.partial(near_kernel, row_total, col_total, part)...]
    unnamed x17 -> x19, local copies, waits for them, and re-layouts: 2.36 us -> 0.9 us
    pallas_call x1, Pallas kernels: 1.66 us -> 0.33 us  [pack_band(): pl.pallas_call(functools.partial(pack_kernel, col_total), out_shape=jax.S...]
    ppermute x19 -> x14, waiting for transfers between devices: 14.1 us -> 15.2 us  [swap(): return lax.ppermute(values, axis, [(i, i ^ flip) for i in range(size)])]
  transfers between devices with their start and end apart: 19 -> 14, of which waited for: 7 -> 9; matrix products, arithmetic and copies ran while one was open for 5% -> 5% of each run, Pallas kernels for 0% -> 9%
where the time goes in v2:
time: 49.7 us; the launch traced here: 49.6 us
  starting transfers between devices  15.9 us (32%)
  waiting for transfers between devices  15.2 us (31%)
  Pallas kernels  12.9 us (26%)
  local copies, waits for them, and re-layouts  2.96 us (6%)
  other arithmetic  1.81 us (4%)
  between operations  0.86 us (2%)
    ppermute x14, starting transfers between devices, swap(): return lax.ppermute(values, axis, [(i, i ^ flip) for i in range(size)])  15.9 us
    ppermute x14, waiting for transfers between devices, swap(): return lax.ppermute(values, axis, [(i, i ^ flip) for i in range(size)])  15.2 us
    pallas_call x3, Pallas kernels, near_part(): pl.pallas_call(functools.partial(near_kernel, row_total, col_total, part)...  12.4 us
    unnamed x1, other arithmetic  1.66 us
    reshape x1, local copies, waits for them, and re-layouts, finish(): return field.reshape(1, LIVE * GX)  1.43 us
  transfers between devices with their start and end apart: 14, of which 9 were waited for; matrix products, arithmetic and copies ran while one was open for 5% of the time, Pallas kernels for 9%

profile of v2, /device:TPU:0, one launch (start us, length us, event | category | flops | bytes accessed | tf_op | source)
XLA Modules:
  0.0 49.6 jit_solution(9964759468232762672)
XLA Ops:
  0.7 0.7 %copy-done.8 = s32[1,8,2]{1,2,0:T(2,128)S(1)} copy-done((s32[1,8,2]{1,2,0:T(2,128)S(1)}, s32[1,8,2]{1,2,0:T(2,128)}, u32[]{:S(2)}) %copy-start.8) | copy-done | bytes 88
  1.3 0.1 copy.13
  1.5 0.5 collective-permute-start
  1.9 1.7 %reduce = bf16[64000]{0:T(1024)(128)(2,1)S(1)} reduce(bf16[1,64000]{1,0:T(2,128)(2,1)} %param.11, bf16[]{:T(256)} %constant.29), dimensions={0}, to_apply=%param.11.reduce_sub_computation | reduce | bytes 256002 | tf_op args[0]
  3.6 0.6 %reshape.13.band_ref = bf16[1600,40]{1,0:T(8,128)(2,1)S(1)} reshape(bf16[64000]{0:T(1024)(128)(2,1)S(1)} %reduce) | data formatting | bytes 256000 | tf_op jit(solution)/shard_map/reshape | solution.py:426
  4.2 0.1 copy-done
  4.4 0.3 pack_band.1.refs_0_
  4.8 2.6 %collective-permute-start.4 = (bf16[1,560,128]{2,1,0:T(8,128)(2,1)S(1)}, bf16[1,560,128]{2,1,0:T(8,128)(2,1)S(1)}, u32[]{:S(2)}, u32[]{:S(2)}) collective-permute-start(bf16[1,560,128]{2,1,0:T(8,128)(2,1)S(1)} %pack_band.1.refs_0_), channel_id=1, source_target_pairs={{0,2},{1,3},{2,0},{3,1},{4,6},{5,7},{6,4},{7,5},{8,10},{9,11},{10,... | collective-permute-start | bytes 430088 | tf_op jit(solution)/shard_map/ppermute | solution.py:407
  7.3 1.5 %collective-permute-start.3 = (bf16[1,560,128]{2,1,0:T(8,128)(2,1)S(1)}, bf16[1,560,128]{2,1,0:T(8,128)(2,1)S(1)}, u32[]{:S(2)}, u32[]{:S(2)}) collective-permute-start(bf16[1,560,128]{2,1,0:T(8,128)(2,1)S(1)} %pack_band.1.refs_0_), channel_id=1, source_target_pairs={{0,4},{4,0},{8,12},{12,8},{16,20},{20,16},{24,28},{28,24},{1,5},{5... | collective-permute-start | bytes 430088 | tf_op jit(solution)/shard_map/ppermute | solution.py:407
  8.8 1.6 %collective-permute-start.2 = (bf16[1,560,128]{2,1,0:T(8,128)(2,1)S(1)}, bf16[1,560,128]{2,1,0:T(8,128)(2,1)S(1)}, u32[]{:S(2)}, u32[]{:S(2)}) collective-permute-start(bf16[1,560,128]{2,1,0:T(8,128)(2,1)S(1)} %pack_band.1.refs_0_), channel_id=1, source_target_pairs={{0,8},{4,12},{8,0},{12,4},{16,24},{20,28},{24,16},{28,20},{1,9},{5... | collective-permute-start | bytes 430088 | tf_op jit(solution)/shard_map/ppermute | solution.py:407
  10.4 2.6 %collective-permute-start.1 = (bf16[1,560,128]{2,1,0:T(8,128)(2,1)S(1)}, bf16[1,560,128]{2,1,0:T(8,128)(2,1)S(1)}, u32[]{:S(2)}, u32[]{:S(2)}) collective-permute-start(bf16[1,560,128]{2,1,0:T(8,128)(2,1)S(1)} %pack_band.1.refs_0_), channel_id=1, source_target_pairs={{0,16},{4,20},{8,24},{12,28},{16,0},{20,4},{24,8},{28,12},{1,17},{... | collective-permute-start | bytes 430088 | tf_op jit(solution)/shard_map/ppermute | solution.py:407
  13.0 0.2 collective-permute-done.3.refs_3_
  13.2 3.9 %collective-permute-done.2.refs_2_ = bf16[1,560,128]{2,1,0:T(8,128)(2,1)S(1)} collective-permute-done((bf16[1,560,128]{2,1,0:T(8,128)(2,1)S(1)}, bf16[1,560,128]{2,1,0:T(8,128)(2,1)S(1)}, u32[]{:S(2)}, u32[]{:S(2)}) %collective-permute-start.2) | collective-permute-done | bytes 143392 | tf_op jit(solution)/shard_map/ppermute | solution.py:407
  17.1 2.7 %collective-permute-done.1.refs_1_ = bf16[1,560,128]{2,1,0:T(8,128)(2,1)S(1)} collective-permute-done((bf16[1,560,128]{2,1,0:T(8,128)(2,1)S(1)}, bf16[1,560,128]{2,1,0:T(8,128)(2,1)S(1)}, u32[]{:S(2)}, u32[]{:S(2)}) %collective-permute-start.1) | collective-permute-done | bytes 143392 | tf_op jit(solution)/shard_map/ppermute | solution.py:407
  19.8 0.5 %collective-permute-start.8 = (bf16[2,560,128]{2,1,0:T(8,128)(2,1)S(1)}, bf16[2,560,128]{2,1,0:T(8,128)(2,1)S(1)}, u32[]{:S(2)}, u32[]{:S(2)}) collective-permute-start(bf16[2,560,128]{2,1,0:T(8,128)(2,1)S(1)} %get-tuple-element.31), channel_id=1, source_target_pairs={{0,8},{4,12},{8,0},{12,4},{16,24},{20,28},{24,16},{28,20},{1,9},{5... | collective-permute-start | bytes 860168 | tf_op jit(solution)/shard_map/ppermute | solution.py:407
  20.4 0.5 %collective-permute-start.7 = (bf16[2,560,128]{2,1,0:T(8,128)(2,1)S(1)}, bf16[2,560,128]{2,1,0:T(8,128)(2,1)S(1)}, u32[]{:S(2)}, u32[]{:S(2)}) collective-permute-start(bf16[2,560,128]{2,1,0:T(8,128)(2,1)S(1)} %get-tuple-element.32), channel_id=1, source_target_pairs={{0,4},{4,0},{8,12},{12,8},{16,20},{20,16},{24,28},{28,24},{1,5},{5... | collective-permute-start | bytes 860168 | tf_op jit(solution)/shard_map/ppermute | solution.py:407
  20.9 0.5 %collective-permute-start.6 = (bf16[2,560,128]{2,1,0:T(8,128)(2,1)S(1)}, bf16[2,560,128]{2,1,0:T(8,128)(2,1)S(1)}, u32[]{:S(2)}, u32[]{:S(2)}) collective-permute-start(bf16[2,560,128]{2,1,0:T(8,128)(2,1)S(1)} %get-tuple-element.33), channel_id=1, source_target_pairs={{0,2},{1,3},{2,0},{3,1},{4,6},{5,7},{6,4},{7,5},{8,10},{9,11},{10,... | collective-permute-start | bytes 860168 | tf_op jit(solution)/shard_map/ppermute | solution.py:407
  21.5 1.1 %solve_part.3 = (f32[1680,128]{1,0:T(8,128)S(1)}, f32[1680,128]{1,0:T(8,128)S(1)}, f32[1680,128]{1,0:T(8,128)S(1)}, f32[1680,128]{1,0:T(8,128)S(1)}) custom-call(bf16[1,560,128]{2,1,0:T(8,128)(2,1)S(1)} %pack_band.1.refs_0_, bf16[1,560,128]{2,1,0:T(8,128)(2,1)S(1)} %collective-permute-done.1.refs_1_, ...), custom_call_target="tpu_custom_call" | custom-call | flops 4000000000 | bytes 20000000 | tf_op jit(solution)/shard_map/solve_part/pallas_call | solution.py:459
  22.5 4.0 %collective-permute-done.8.refs_7_ = bf16[2,560,128]{2,1,0:T(8,128)(2,1)S(1)} collective-permute-done((bf16[2,560,128]{2,1,0:T(8,128)(2,1)S(1)}, bf16[2,560,128]{2,1,0:T(8,128)(2,1)S(1)}, u32[]{:S(2)}, u32[]{:S(2)}) %collective-permute-start.8) | collective-permute-done | bytes 286752 | tf_op jit(solution)/shard_map/ppermute | solution.py:407
  26.5 1.3 %collective-permute-done.7.refs_6_ = bf16[2,560,128]{2,1,0:T(8,128)(2,1)S(1)} collective-permute-done((bf16[2,560,128]{2,1,0:T(8,128)(2,1)S(1)}, bf16[2,560,128]{2,1,0:T(8,128)(2,1)S(1)}, u32[]{:S(2)}, u32[]{:S(2)}) %collective-permute-start.7) | collective-permute-done | bytes 286752 | tf_op jit(solution)/shard_map/ppermute | solution.py:407
  27.8 0.2 collective-permute-done.6.refs_5_
  28.1 0.6 %collective-permute-start.9 = (bf16[1,560,128]{2,1,0:T(8,128)(2,1)S(1)}, bf16[1,560,128]{2,1,0:T(8,128)(2,1)S(1)}, u32[]{:S(2)}, u32[]{:S(2)}) collective-permute-start(bf16[1,560,128]{2,1,0:T(8,128)(2,1)S(1)} %slice.6), channel_id=1, source_target_pairs={{0,2},{1,3},{2,0},{3,1},{4,6},{5,7},{6,4},{7,5},{8,10},{9,11},{10,... | collective-permute-start | bytes 430088 | tf_op jit(solution)/shard_map/ppermute | solution.py:407
  28.7 1.6 %collective-permute-start.10 = (bf16[1,560,128]{2,1,0:T(8,128)(2,1)S(1)}, bf16[1,560,128]{2,1,0:T(8,128)(2,1)S(1)}, u32[]{:S(2)}, u32[]{:S(2)}) collective-permute-start(bf16[1,560,128]{2,1,0:T(8,128)(2,1)S(1)} %slice.7), channel_id=1, source_target_pairs={{0,4},{4,0},{8,12},{12,8},{16,20},{20,16},{24,28},{28,24},{1,5},{5... | collective-permute-start | bytes 430088 | tf_op jit(solution)/shard_map/ppermute | solution.py:407
  30.3 1.9 %collective-permute-start.11 = (bf16[2,560,128]{2,1,0:T(8,128)(2,1)S(1)}, bf16[2,560,128]{2,1,0:T(8,128)(2,1)S(1)}, u32[]{:S(2)}, u32[]{:S(2)}) collective-permute-start(bf16[2,560,128]{2,1,0:T(8,128)(2,1)S(1)} %collective-permute-done.7.refs_6_), channel_id=1, source_target_pairs={{0,8},{4,12},{8,0},{12,4},{16,24},{20,28},{24,16},{28,20},{1,9},{5... | collective-permute-start | bytes 860168 | tf_op jit(solution)/shard_map/ppermute | solution.py:407
  32.1 1.1 %collective-permute-done.9.refs_8_ = bf16[1,560,128]{2,1,0:T(8,128)(2,1)S(1)} collective-permute-done((bf16[1,560,128]{2,1,0:T(8,128)(2,1)S(1)}, bf16[1,560,128]{2,1,0:T(8,128)(2,1)S(1)}, u32[]{:S(2)}, u32[]{:S(2)}) %collective-permute-start.9) | collective-permute-done | bytes 143392 | tf_op jit(solution)/shard_map/ppermute | solution.py:407
  33.2 1.5 %collective-permute-start.12 = (bf16[1,560,128]{2,1,0:T(8,128)(2,1)S(1)}, bf16[1,560,128]{2,1,0:T(8,128)(2,1)S(1)}, u32[]{:S(2)}, u32[]{:S(2)}) collective-permute-start(bf16[1,560,128]{2,1,0:T(8,128)(2,1)S(1)} %collective-permute-done.9.refs_8_), channel_id=1, source_target_pairs={{0,4},{4,0},{8,12},{12,8},{16,20},{20,16},{24,28},{28,24},{1,5},{5... | collective-permute-start | bytes 430088 | tf_op jit(solution)/shard_map/ppermute | solution.py:407
  34.8 3.3 %solve_part.4 = (f32[1680,128]{1,0:T(8,128)S(1)}, f32[1680,128]{1,0:T(8,128)S(1)}) custom-call(bf16[1,560,128]{2,1,0:T(8,128)(2,1)S(1)} %pack_band.1.refs_0_, bf16[1,560,128]{2,1,0:T(8,128)(2,1)S(1)} %collective-permute-done.1.refs_1_, bf16[1,560,128]{2,1,0:T(8,128)(2,1)S(1)} %collective-permute-done.2.refs_2_, ...), custom_call_target="tpu_custom_call" | custom-call | flops 4000000000 | bytes 20000000 | tf_op jit(solution)/shard_map/solve_part/pallas_call | solution.py:459
  38.1 0.2 collective-permute-done.12.refs_11_
  38.3 8.0 %solve_part.5 = (f32[560,128]{1,0:T(8,128)S(1)}, f32[560,128]{1,0:T(8,128)S(1)}) custom-call(bf16[1,560,128]{2,1,0:T(8,128)(2,1)S(1)} %pack_band.1.refs_0_, bf16[1,560,128]{2,1,0:T(8,128)(2,1)S(1)} %collective-permute-done.1.refs_1_, bf16[1,560,128]{2,1,0:T(8,128)(2,1)S(1)} %collective-permute-done.2.refs_2_, ...), custom_call_target="tpu_custom_call" | custom-call | flops 4000000000 | bytes 20000000 | tf_op jit(solution)/shard_map/solve_part/pallas_call | solution.py:459
  46.4 1.6 %collective-permute-done.13.part_ref = f32[560,128]{1,0:T(8,128)S(1)} collective-permute-done((f32[560,128]{1,0:T(8,128)S(1)}, f32[560,128]{1,0:T(8,128)S(1)}, u32[]{:S(2)}, u32[]{:S(2)}) %collective-permute-start.13) | collective-permute-done | bytes 286752 | tf_op jit(solution)/shard_map/ppermute | solution.py:407
  48.0 0.2 add_parts.1
  48.2 1.4 %reshape.14 = f32[1,64000]{1,0:T(1,128)} reshape(f32[1600,40]{1,0:T(8,128)S(1)} %add_parts.1) | data formatting | bytes 512000 | tf_op jit(solution)/shard_map/reshape | solution.py:438
  (28 shorter events, 0.3 us)
Async XLA Ops:
  0.7 0.7 %copy-start.8 = (s32[1,8,2]{1,2,0:T(2,128)S(1)}, s32[1,8,2]{1,2,0:T(2,128)}, u32[]{:S(2)}) copy-start(s32[1,8,2]{1,2,0:T(2,128)} %param.12) | copy-start | bytes 196
  1.5 2.7 %collective-permute-start = (s32[1,8,2]{2,1,0:T(8,128)S(1)}, s32[1,8,2]{2,1,0:T(8,128)S(1)}, u32[]{:S(2)}, u32[]{:S(2)}) collective-permute-start(s32[1,8,2]{2,1,0:T(8,128)S(1)} %broadcast_select_fusion.rest_0_), channel_id=1, source_target_pairs={{0,1},{1,0},{2,3},{3,2},{4,5},{5,4},{6,7},{7,6},{8,9},{9,8},{10,11... | collective-permute-start | bytes 200 | tf_op jit(solution)/shard_map/ppermute | solution.py:407
  3.6 0.8 %copy-start = (bf16[3,40,128]{2,1,0:T(8,128)(2,1)S(1)}, bf16[3,40,128]{2,1,0:T(8,128)(2,1)}, u32[]{:S(2)}) copy-start(bf16[3,40,128]{2,1,0:T(8,128)(2,1)} %constant.18.clone.table_ref) | copy-start | bytes 92164
  4.4 17.0 %copy-start.5 = (bf16[128,384]{1,0:T(8,128)(2,1)S(1)}, bf16[128,384]{1,0:T(8,128)(2,1)}, u32[]{:S(2)}) copy-start(bf16[128,384]{1,0:T(8,128)(2,1)} %constant.20.clone.refs_7_.refs_10_.refs_14_) | copy-start | bytes 294916
  4.4 17.0 %copy-start.7 = (bf16[80,240]{1,0:T(8,128)(2,1)S(1)}, bf16[80,240]{1,0:T(8,128)(2,1)}, u32[]{:S(2)}) copy-start(bf16[80,240]{1,0:T(8,128)(2,1)} %constant.23.clone.refs_10_.refs_13_.refs_17_) | copy-start | bytes 115204
  4.7 16.7 %copy-start.1 = (f32[1600,128]{1,0:T(8,128)S(1)}, f32[1600,128]{1,0:T(8,128)}, u32[]{:S(2)}) copy-start(f32[1600,128]{1,0:T(8,128)} %constant.25.clone.refs_12_.refs_15_.refs_19_) | copy-start | bytes 2457604
  4.7 16.7 %copy-start.2 = (bf16[384,384]{1,0:T(8,128)(2,1)S(1)}, bf16[384,384]{1,0:T(8,128)(2,1)}, u32[]{:S(2)}) copy-start(bf16[384,384]{1,0:T(8,128)(2,1)} %constant.19.clone.refs_6_.refs_9_.refs_13_) | copy-start | bytes 884740
  4.7 16.7 %copy-start.3 = (bf16[256,256]{1,0:T(8,128)(2,1)S(1)}, bf16[256,256]{1,0:T(8,128)(2,1)}, u32[]{:S(2)}) copy-start(bf16[256,256]{1,0:T(8,128)(2,1)} %constant.22.clone.refs_9_.refs_12_.refs_16_) | copy-start | bytes 393220
  4.7 16.7 %copy-start.4 = (bf16[256,256]{1,0:T(8,128)(2,1)S(1)}, bf16[256,256]{1,0:T(8,128)(2,1)}, u32[]{:S(2)}) copy-start(bf16[256,256]{1,0:T(8,128)(2,1)} %constant.21.clone.refs_8_.refs_11_.refs_15_) | copy-start | bytes 393220
  4.7 16.7 %copy-start.6 = (bf16[80,240]{1,0:T(8,128)(2,1)S(1)}, bf16[80,240]{1,0:T(8,128)(2,1)}, u32[]{:S(2)}) copy-start(bf16[80,240]{1,0:T(8,128)(2,1)} %constant.24.clone.refs_11_.refs_14_.refs_18_) | copy-start | bytes 115204
  4.8 8.3 %collective-permute-start.4 = (bf16[1,560,128]{2,1,0:T(8,128)(2,1)S(1)}, bf16[1,560,128]{2,1,0:T(8,128)(2,1)S(1)}, u32[]{:S(2)}, u32[]{:S(2)}) collective-permute-start(bf16[1,560,128]{2,1,0:T(8,128)(2,1)S(1)} %pack_band.1.refs_0_), channel_id=1, source_target_pairs={{0,2},{1,3},{2,0},{3,1},{4,6},{5,7},{6,4},{7,5},{8,10},{9,11},{10,... | collective-permute-start | bytes 430088 | tf_op jit(solution)/shard_map/ppermute | solution.py:407
  7.3 5.9 %collective-permute-start.3 = (bf16[1,560,128]{2,1,0:T(8,128)(2,1)S(1)}, bf16[1,560,128]{2,1,0:T(8,128)(2,1)S(1)}, u32[]{:S(2)}, u32[]{:S(2)}) collective-permute-start(bf16[1,560,128]{2,1,0:T(8,128)(2,1)S(1)} %pack_band.1.refs_0_), channel_id=1, source_target_pairs={{0,4},{4,0},{8,12},{12,8},{16,20},{20,16},{24,28},{28,24},{1,5},{5... | collective-permute-start | bytes 430088 | tf_op jit(solution)/shard_map/ppermute | solution.py:407
  8.8 8.3 %collective-permute-start.2 = (bf16[1,560,128]{2,1,0:T(8,128)(2,1)S(1)}, bf16[1,560,128]{2,1,0:T(8,128)(2,1)S(1)}, u32[]{:S(2)}, u32[]{:S(2)}) collective-permute-start(bf16[1,560,128]{2,1,0:T(8,128)(2,1)S(1)} %pack_band.1.refs_0_), channel_id=1, source_target_pairs={{0,8},{4,12},{8,0},{12,4},{16,24},{20,28},{24,16},{28,20},{1,9},{5... | collective-permute-start | bytes 430088 | tf_op jit(solution)/shard_map/ppermute | solution.py:407
  10.4 9.3 %collective-permute-start.1 = (bf16[1,560,128]{2,1,0:T(8,128)(2,1)S(1)}, bf16[1,560,128]{2,1,0:T(8,128)(2,1)S(1)}, u32[]{:S(2)}, u32[]{:S(2)}) collective-permute-start(bf16[1,560,128]{2,1,0:T(8,128)(2,1)S(1)} %pack_band.1.refs_0_), channel_id=1, source_target_pairs={{0,16},{4,20},{8,24},{12,28},{16,0},{20,4},{24,8},{28,12},{1,17},{... | collective-permute-start | bytes 430088 | tf_op jit(solution)/shard_map/ppermute | solution.py:407
  13.0 8.4 %collective-permute-start.5 = (bf16[1,560,128]{2,1,0:T(8,128)(2,1)S(1)}, bf16[1,560,128]{2,1,0:T(8,128)(2,1)S(1)}, u32[]{:S(2)}, u32[]{:S(2)}) collective-permute-start(bf16[1,560,128]{2,1,0:T(8,128)(2,1)S(1)} %pack_band.1.refs_0_), channel_id=1, source_target_pairs={{0,1},{1,0},{2,3},{3,2},{4,5},{5,4},{6,7},{7,6},{8,9},{9,8},{10,11... | collective-permute-start | bytes 430088 | tf_op jit(solution)/shard_map/ppermute | solution.py:407
  19.8 6.7 %collective-permute-start.8 = (bf16[2,560,128]{2,1,0:T(8,128)(2,1)S(1)}, bf16[2,560,128]{2,1,0:T(8,128)(2,1)S(1)}, u32[]{:S(2)}, u32[]{:S(2)}) collective-permute-start(bf16[2,560,128]{2,1,0:T(8,128)(2,1)S(1)} %get-tuple-element.31), channel_id=1, source_target_pairs={{0,8},{4,12},{8,0},{12,4},{16,24},{20,28},{24,16},{28,20},{1,9},{5... | collective-permute-start | bytes 860168 | tf_op jit(solution)/shard_map/ppermute | solution.py:407
  20.4 7.5 %collective-permute-start.7 = (bf16[2,560,128]{2,1,0:T(8,128)(2,1)S(1)}, bf16[2,560,128]{2,1,0:T(8,128)(2,1)S(1)}, u32[]{:S(2)}, u32[]{:S(2)}) collective-permute-start(bf16[2,560,128]{2,1,0:T(8,128)(2,1)S(1)} %get-tuple-element.32), channel_id=1, source_target_pairs={{0,4},{4,0},{8,12},{12,8},{16,20},{20,16},{24,28},{28,24},{1,5},{5... | collective-permute-start | bytes 860168 | tf_op jit(solution)/shard_map/ppermute | solution.py:407
  20.9 7.2 %collective-permute-start.6 = (bf16[2,560,128]{2,1,0:T(8,128)(2,1)S(1)}, bf16[2,560,128]{2,1,0:T(8,128)(2,1)S(1)}, u32[]{:S(2)}, u32[]{:S(2)}) collective-permute-start(bf16[2,560,128]{2,1,0:T(8,128)(2,1)S(1)} %get-tuple-element.33), channel_id=1, source_target_pairs={{0,2},{1,3},{2,0},{3,1},{4,6},{5,7},{6,4},{7,5},{8,10},{9,11},{10,... | collective-permute-start | bytes 860168 | tf_op jit(solution)/shard_map/ppermute | solution.py:407
  28.1 5.2 %collective-permute-start.9 = (bf16[1,560,128]{2,1,0:T(8,128)(2,1)S(1)}, bf16[1,560,128]{2,1,0:T(8,128)(2,1)S(1)}, u32[]{:S(2)}, u32[]{:S(2)}) collective-permute-start(bf16[1,560,128]{2,1,0:T(8,128)(2,1)S(1)} %slice.6), channel_id=1, source_target_pairs={{0,2},{1,3},{2,0},{3,1},{4,6},{5,7},{6,4},{7,5},{8,10},{9,11},{10,... | collective-permute-start | bytes 430088 | tf_op jit(solution)/shard_map/ppermute | solution.py:407
  28.7 9.4 %collective-permute-start.10 = (bf16[1,560,128]{2,1,0:T(8,128)(2,1)S(1)}, bf16[1,560,128]{2,1,0:T(8,128)(2,1)S(1)}, u32[]{:S(2)}, u32[]{:S(2)}) collective-permute-start(bf16[1,560,128]{2,1,0:T(8,128)(2,1)S(1)} %slice.7), channel_id=1, source_target_pairs={{0,4},{4,0},{8,12},{12,8},{16,20},{20,16},{24,28},{28,24},{1,5},{5... | collective-permute-start | bytes 430088 | tf_op jit(solution)/shard_map/ppermute | solution.py:407
  30.3 7.8 %collective-permute-start.11 = (bf16[2,560,128]{2,1,0:T(8,128)(2,1)S(1)}, bf16[2,560,128]{2,1,0:T(8,128)(2,1)S(1)}, u32[]{:S(2)}, u32[]{:S(2)}) collective-permute-start(bf16[2,560,128]{2,1,0:T(8,128)(2,1)S(1)} %collective-permute-done.7.refs_6_), channel_id=1, source_target_pairs={{0,8},{4,12},{8,0},{12,4},{16,24},{20,28},{24,16},{28,20},{1,9},{5... | collective-permute-start | bytes 860168 | tf_op jit(solution)/shard_map/ppermute | solution.py:407
  33.2 5.1 %collective-permute-start.12 = (bf16[1,560,128]{2,1,0:T(8,128)(2,1)S(1)}, bf16[1,560,128]{2,1,0:T(8,128)(2,1)S(1)}, u32[]{:S(2)}, u32[]{:S(2)}) collective-permute-start(bf16[1,560,128]{2,1,0:T(8,128)(2,1)S(1)} %collective-permute-done.9.refs_8_), channel_id=1, source_target_pairs={{0,4},{4,0},{8,12},{12,8},{16,20},{20,16},{24,28},{28,24},{1,5},{5... | collective-permute-start | bytes 430088 | tf_op jit(solution)/shard_map/ppermute | solution.py:407
  46.3 1.6 %collective-permute-start.13 = (f32[560,128]{1,0:T(8,128)S(1)}, f32[560,128]{1,0:T(8,128)S(1)}, u32[]{:S(2)}, u32[]{:S(2)}) collective-permute-start(f32[560,128]{1,0:T(8,128)S(1)} %get-tuple-element.30), channel_id=1, source_target_pairs={{0,1},{1,0},{2,3},{3,2},{4,5},{5,4},{6,7},{7,6},{8,9},{9,8},{10,11... | collective-permute-start | bytes 860168 | tf_op jit(solution)/shard_map/ppermute | solution.py:407

commit v3 on v2

--- a/solution.py
+++ b/solution.py
@@ -18,6 +18,9 @@
 ROWS = SIDE * PACK
 LIVE = GX * GX
 SPARE = SIDE * GX
+FLAT = LIVE * GX // LANES
+CHUNK = PACK // 16
+FLAT_ROWS = SIDE * CHUNK * 5 + 8
 DUO = 2 * GX
 QUAD = 4 * GX
 GROUP = 10
@@ -78,13 +81,6 @@
         out[row + z, col + z] = 1.0
 
 
-def pack_table():
-    out = np.zeros((SIDE, GX, LANES), np.float32)
-    for third in range(SIDE):
-        place(out[third], 0, third * GX)
-    return out.astype(ml_dtypes.bfloat16)
-
-
 def spread_table():
     out = np.zeros((SIDE * LANES, SIDE * LANES), np.float32)
     for third in range(SIDE):
@@ -162,21 +158,38 @@
     return lax.dot_general(first, second, (((0,), (0,)), ((), ())), preferred_element_type=F32)
 
 
-def pack_kernel(col_total, band_ref, table_ref, *rest):
-    out_ref = rest[-1]
-    total = None
-    for third in range(SIDE):
-        rows = min(PACK, LIVE - third * PACK)
-        piece = dot(band_ref[pl.ds(third * PACK, rows), :], table_ref[third])
-        if rows < PACK:
-            piece = jnp.concatenate([piece, jnp.zeros((PACK - rows, LANES), F32)], axis=0)
-        total = piece if total is None else total + piece
-    if len(rest) > 1:
-        counts = sum(count_vector(ref, k * col_total) for k, ref in enumerate(rest[:-1]))
-        counts = counts[:16]
-        empty = jnp.zeros((PACK - counts.shape[0], LANES), F32)
-        total = total + jnp.concatenate([counts, empty], axis=0)
-    out_ref[0] = total.astype(BF16)
+def unroll_rows(copy):
+    for k in range(FLAT):
+        copy(k, slice(k * LANES, (k + 1) * LANES))
+
+
+def pack_kernel(col_total, band_ref, *rest):
+    *list_refs, out_ref, flat_ref, wide_ref = rest
+
+    def to_rows(k, lanes):
+        flat_ref[k : k + 1, :] = band_ref[0:1, lanes].astype(F32)
+
+    unroll_rows(to_rows)
+    unused = FLAT_ROWS - FLAT
+    flat_ref[FLAT:FLAT_ROWS, :] = jnp.zeros((unused, LANES), F32)
+    lane = lax.broadcasted_iota(jnp.int32, (1, LANES), 1)
+    for q in range(16):
+        row, offset = divmod(q * GX, LANES)
+        packed = jnp.zeros((CHUNK, LANES), F32)
+        for third in range(SIDE):
+            start = third * CHUNK * 5 + row
+            values = flat_ref[pl.ds(start, CHUNK, stride=5), :]
+            if offset + GX > LANES:
+                after = flat_ref[pl.ds(start + 1, CHUNK, stride=5), :]
+                values = jnp.where(lane >= offset, values, after)
+            shift = (third * GX - offset) % LANES
+            values = pltpu.roll(values, shift, 1) if shift else values
+            packed = jnp.where(lane // GX == third, values, packed)
+        wide_ref[pl.ds(q, CHUNK, stride=16), :] = packed
+    if list_refs:
+        counts = sum(count_vector(ref, k * col_total) for k, ref in enumerate(list_refs))
+        wide_ref[0:16, :] = wide_ref[0:16, :] + counts[:16]
+    out_ref[0] = wide_ref[...].astype(BF16)
 
 
 def spread_waves(own_bands, repeat_ref, wave_refs):
@@ -367,13 +380,27 @@
     pack_fields(sum_refs, out_refs)
 
 
-def finish_kernel(own_ref, part_ref, out_ref):
+def finish_kernel(own_ref, part_ref, out_ref, wide_ref, flat_ref):
+    wide_ref[...] = own_ref[...] + part_ref[...]
+    lane = lax.broadcasted_iota(jnp.int32, (1, LANES), 1)
     for third in range(SIDE):
-        rows = min(PACK, LIVE - third * PACK)
-        values = own_ref[pl.ds(0, rows), :] + part_ref[pl.ds(0, rows), :]
-        if third:
-            values = pltpu.roll(values, LANES - third * GX, 1)
-        out_ref[pl.ds(third * PACK, rows), :] = values[:, :GX]
+        rows = min(CHUNK, LIVE // 16 - third * CHUNK)
+        flat = [jnp.zeros((rows, LANES), F32)] * 5
+        for q in range(16):
+            row, offset = divmod(q * GX, LANES)
+            shift = (offset - third * GX) % LANES
+            values = wide_ref[pl.ds(q, rows, stride=16), :]
+            values = pltpu.roll(values, shift, 1) if shift else values
+            flat[row] = jnp.where(lane >= offset, values, flat[row])
+            if offset + GX > LANES:
+                flat[row + 1] = jnp.where(lane < offset + GX - LANES, values, flat[row + 1])
+        for row in range(5):
+            flat_ref[pl.ds(third * CHUNK * 5 + row, rows, stride=5), :] = flat[row]
+
+    def to_lanes(k, lanes):
+        out_ref[0:1, lanes] = flat_ref[k : k + 1, :]
+
+    unroll_rows(to_lanes)
 
 
 VMEM_SPEC = pl.BlockSpec(memory_space=pltpu.VMEM)
@@ -415,34 +442,35 @@
     return jnp.sum((first & second & live[:, None, None]).astype(F32), axis=0)
 
 
-def pack_band(orbitals, col_total, extras):
+def pack_band(orbitals, col_total, lists):
     return pl.pallas_call(
         functools.partial(pack_kernel, col_total),
         out_shape=jax.ShapeDtypeStruct((1, PACK, LANES), BF16),
-        in_specs=[VMEM_SPEC] * (2 + len(extras)),
+        in_specs=[VMEM_SPEC] * (1 + len(lists)),
         out_specs=VMEM_SPEC,
+        scratch_shapes=[pltpu.VMEM((FLAT_ROWS, LANES), F32), pltpu.VMEM((PACK, LANES), F32)],
         compiler_params=PARAMS,
         name="pack_band",
-    )(orbitals.reshape(LIVE, GX), jnp.asarray(pack_table()), *extras)
+    )(orbitals, *lists)
 
 
 def finish(own, part):
-    field = pl.pallas_call(
+    return pl.pallas_call(
         finish_kernel,
-        out_shape=jax.ShapeDtypeStruct((LIVE, GX), F32),
+        out_shape=jax.ShapeDtypeStruct((1, LIVE * GX), F32),
         in_specs=[VMEM_SPEC] * 2,
         out_specs=VMEM_SPEC,
+        scratch_shapes=[pltpu.VMEM((PACK, LANES), F32), pltpu.VMEM((FLAT_ROWS, LANES), F32)],
         compiler_params=PARAMS,
         name="add_parts",
     )(own, part)
-    return field.reshape(1, LIVE * GX)
 
 
 NEAR = (8, 4)
 STAGES = (
     (((0, 0),), ((4, 0),), ((2, 0),), ((1, 0),), ((0, 2),)),
-    (((4, 2), (2, 2)), ((5, 0), (1, 2)), ((6, 0), (3, 0))),
-    (((6, 2),), ((5, 2),), ((7, 0), (3, 2)), ((7, 2),)),
+    (((4, 2), (2, 2)), ((5, 0), (1, 2)), ((6, 0), (3, 0)), ((6, 2),), ((5, 2),)),
+    (((7, 0), (3, 2)), ((7, 2),)),
 )
 CAPS = (2, 2)
 
@@ -484,7 +512,7 @@
     live = lax.iota(jnp.int32, pair_list.shape[1])[None, :, None] < pair_count[0]
     pairs = jnp.where(live, pair_list, -row_total * col_total)
     own = pack_band(orbitals, col_total, [pairs, col_swap(pairs, 1)])
-    w, z, y, x = row_swap(own, 4), row_swap(own, 2), row_swap(own, 1), col_swap(own, 2)
+    x, y, z, w = col_swap(own, 2), row_swap(own, 1), row_swap(own, 2), row_swap(own, 4)
     mate = col_swap(own, 1)
     over_x, over_y, over_z = col_swap(both(w, z), 2), row_swap(both(w, x), 1), row_swap(both(w, y), 2)
     tables = [jnp.asarray(table) for table in solve_tables()]
@@ -496,7 +524,7 @@
     wxy = row_swap(over_x[:1], 1)
     wyz_xyz = row_swap(over_y, 2)
     wzxy = row_swap(wzx, 1)
-    arrivals = ((over_x, over_y, over_z), (wzx, wxy, wyz_xyz, wzxy))
+    arrivals = ((over_x, over_y, over_z, wzx, wxy), (wyz_xyz, wzxy))
     for part, arrived in enumerate(arrivals, 1):
         blocks += arrived
         operands = [*blocks, mate, *tables, *waves, sum0, sum1]

time: 49.7 us -> 47.2 us (0.950)
  Pallas kernels: 12.9 us -> 16.2 us
  waiting for transfers between devices: 15.2 us -> 12 us
  other arithmetic: 1.81 us -> 0.15 us
  local copies, waits for them, and re-layouts: 2.96 us -> 1.76 us
  starting transfers between devices: 15.9 us -> 16.5 us
    ppermute x14, waiting for transfers between devices: 15.2 us -> 12 us  [swap(): return lax.ppermute(values, axis, [(i, i ^ flip) for i in range(size)])]
    pallas_call x3, Pallas kernels: 12.4 us -> 14.6 us  [near_part(): pl.pallas_call(functools.partial(near_kernel, row_total, col_total, part)...]
    reshape x2 -> x0, local copies, waits for them, and re-layouts: 2.04 us -> none  [the longest x1 1.43 us: finish(): return field.reshape(1, LIVE * GX)]
    unnamed x1 -> x0, other arithmetic: 1.66 us -> none
    pallas_call x1, Pallas kernels: 0.21 us -> 1.19 us  [finish(): pl.pallas_call(finish_kernel, out_shape=jax.ShapeDtypeStruct((1, LIVE * G...]
    unnamed x19 -> x17, local copies, waits for them, and re-layouts: 0.9 us -> 1.74 us
    ppermute x14, starting transfers between devices: 15.9 us -> 16.5 us  [swap(): return lax.ppermute(values, axis, [(i, i ^ flip) for i in range(size)])]
  transfers between devices with their start and end apart: 14 -> 14, of which waited for: 9 -> 10; matrix products, arithmetic and copies ran while one was open for 5% -> 0% of each run, Pallas kernels for 9% -> 20%
where the time goes in v3:
time: 47.2 us; the launch traced here: 47.4 us
  starting transfers between devices  16.5 us (35%)
  Pallas kernels  16.2 us (34%)
  waiting for transfers between devices  12 us (25%)
  local copies, waits for them, and re-layouts  1.76 us (4%)
  between operations  0.82 us (2%)
    ppermute x14, starting transfers between devices, swap(): return lax.ppermute(values, axis, [(i, i ^ flip) for i in range(size)])  16.5 us
    pallas_call x3, Pallas kernels, near_part(): pl.pallas_call(functools.partial(near_kernel, row_total, col_total, part)...  14.6 us
    ppermute x14, waiting for transfers between devices, swap(): return lax.ppermute(values, axis, [(i, i ^ flip) for i in range(size)])  12 us
    unnamed x17, local copies, waits for them, and re-layouts  1.74 us
    pallas_call x1, Pallas kernels, finish(): pl.pallas_call(finish_kernel, out_shape=jax.ShapeDtypeStruct((1, LIVE * G...  1.19 us
  transfers between devices with their start and end apart: 14, of which 10 were waited for; matrix products, arithmetic and copies ran while one was open for 0% of the time, Pallas kernels for 20%

profile of v3, /device:TPU:0, one launch (start us, length us, event | category | flops | bytes accessed | tf_op | source)
XLA Modules:
  0.0 47.4 jit_solution(7186082520139623508)
XLA Ops:
  0.0 0.8 %copy.11 = s32[1,8,2]{2,1,0:T(8,128)S(1)} copy(s32[1,8,2]{1,2,0:T(2,128)} %param.11) | data formatting | bytes 128 | tf_op args[1]
  1.4 0.1 broadcast_select_fusion.rest_0_
  1.5 0.5 collective-permute-start
  1.9 0.8 %collective-permute-done.rest_1_ = s32[1,8,2]{2,1,0:T(8,128)S(1)} collective-permute-done((s32[1,8,2]{2,1,0:T(8,128)S(1)}, s32[1,8,2]{2,1,0:T(8,128)S(1)}, u32[]{:S(2)}, u32[]{:S(2)}) %collective-permute-start) | collective-permute-done | bytes 96 | tf_op jit(solution)/shard_map/ppermute | solution.py:434
  2.8 0.9 %copy-done = bf16[1,64000]{1,0:T(2,128)(2,1)S(1)} copy-done((bf16[1,64000]{1,0:T(2,128)(2,1)S(1)}, bf16[1,64000]{1,0:T(2,128)(2,1)}, u32[]{:S(2)}) %copy-start) | copy-done | bytes 128024
  3.7 0.4 pack_band.1.refs_0_
  4.2 4.0 %collective-permute-start.1 = (bf16[1,560,128]{2,1,0:T(8,128)(2,1)S(1)}, bf16[1,560,128]{2,1,0:T(8,128)(2,1)S(1)}, u32[]{:S(2)}, u32[]{:S(2)}) collective-permute-start(bf16[1,560,128]{2,1,0:T(8,128)(2,1)S(1)} %pack_band.1.refs_0_), channel_id=1, source_target_pairs={{0,16},{4,20},{8,24},{12,28},{16,0},{20,4},{24,8},{28,12},{1,17},{... | collective-permute-start | bytes 430088 | tf_op jit(solution)/shard_map/ppermute | solution.py:434
  8.2 1.6 %collective-permute-start.2 = (bf16[1,560,128]{2,1,0:T(8,128)(2,1)S(1)}, bf16[1,560,128]{2,1,0:T(8,128)(2,1)S(1)}, u32[]{:S(2)}, u32[]{:S(2)}) collective-permute-start(bf16[1,560,128]{2,1,0:T(8,128)(2,1)S(1)} %pack_band.1.refs_0_), channel_id=1, source_target_pairs={{0,8},{4,12},{8,0},{12,4},{16,24},{20,28},{24,16},{28,20},{1,9},{5... | collective-permute-start | bytes 430088 | tf_op jit(solution)/shard_map/ppermute | solution.py:434
  9.8 1.5 %collective-permute-start.3 = (bf16[1,560,128]{2,1,0:T(8,128)(2,1)S(1)}, bf16[1,560,128]{2,1,0:T(8,128)(2,1)S(1)}, u32[]{:S(2)}, u32[]{:S(2)}) collective-permute-start(bf16[1,560,128]{2,1,0:T(8,128)(2,1)S(1)} %pack_band.1.refs_0_), channel_id=1, source_target_pairs={{0,4},{4,0},{8,12},{12,8},{16,20},{20,16},{24,28},{28,24},{1,5},{5... | collective-permute-start | bytes 430088 | tf_op jit(solution)/shard_map/ppermute | solution.py:434
  11.3 1.5 %collective-permute-start.4 = (bf16[1,560,128]{2,1,0:T(8,128)(2,1)S(1)}, bf16[1,560,128]{2,1,0:T(8,128)(2,1)S(1)}, u32[]{:S(2)}, u32[]{:S(2)}) collective-permute-start(bf16[1,560,128]{2,1,0:T(8,128)(2,1)S(1)} %pack_band.1.refs_0_), channel_id=1, source_target_pairs={{0,2},{1,3},{2,0},{3,1},{4,6},{5,7},{6,4},{7,5},{8,10},{9,11},{10,... | collective-permute-start | bytes 430088 | tf_op jit(solution)/shard_map/ppermute | solution.py:434
  12.8 2.7 %collective-permute-done.1.refs_1_ = bf16[1,560,128]{2,1,0:T(8,128)(2,1)S(1)} collective-permute-done((bf16[1,560,128]{2,1,0:T(8,128)(2,1)S(1)}, bf16[1,560,128]{2,1,0:T(8,128)(2,1)S(1)}, u32[]{:S(2)}, u32[]{:S(2)}) %collective-permute-start.1) | collective-permute-done | bytes 143392 | tf_op jit(solution)/shard_map/ppermute | solution.py:434
  15.5 0.2 collective-permute-done.2.refs_2_
  15.7 0.7 %collective-permute-done.4.refs_4_ = bf16[1,560,128]{2,1,0:T(8,128)(2,1)S(1)} collective-permute-done((bf16[1,560,128]{2,1,0:T(8,128)(2,1)S(1)}, bf16[1,560,128]{2,1,0:T(8,128)(2,1)S(1)}, u32[]{:S(2)}, u32[]{:S(2)}) %collective-permute-start.4) | collective-permute-done | bytes 143392 | tf_op jit(solution)/shard_map/ppermute | solution.py:434
  16.4 0.1 pad_maximum_fusion
  16.5 1.6 %collective-permute-start.6 = (bf16[2,560,128]{2,1,0:T(8,128)(2,1)S(1)}, bf16[2,560,128]{2,1,0:T(8,128)(2,1)S(1)}, u32[]{:S(2)}, u32[]{:S(2)}) collective-permute-start(bf16[2,560,128]{2,1,0:T(8,128)(2,1)S(1)} %get-tuple-element.33), channel_id=1, source_target_pairs={{0,2},{1,3},{2,0},{3,1},{4,6},{5,7},{6,4},{7,5},{8,10},{9,11},{10,... | collective-permute-start | bytes 860168 | tf_op jit(solution)/shard_map/ppermute | solution.py:434
  18.0 0.8 %collective-permute-start.7 = (bf16[2,560,128]{2,1,0:T(8,128)(2,1)S(1)}, bf16[2,560,128]{2,1,0:T(8,128)(2,1)S(1)}, u32[]{:S(2)}, u32[]{:S(2)}) collective-permute-start(bf16[2,560,128]{2,1,0:T(8,128)(2,1)S(1)} %get-tuple-element.32), channel_id=1, source_target_pairs={{0,4},{4,0},{8,12},{12,8},{16,20},{20,16},{24,28},{28,24},{1,5},{5... | collective-permute-start | bytes 860168 | tf_op jit(solution)/shard_map/ppermute | solution.py:434
  18.9 1.4 %collective-permute-start.8 = (bf16[2,560,128]{2,1,0:T(8,128)(2,1)S(1)}, bf16[2,560,128]{2,1,0:T(8,128)(2,1)S(1)}, u32[]{:S(2)}, u32[]{:S(2)}) collective-permute-start(bf16[2,560,128]{2,1,0:T(8,128)(2,1)S(1)} %get-tuple-element.31), channel_id=1, source_target_pairs={{0,8},{4,12},{8,0},{12,4},{16,24},{20,28},{24,16},{28,20},{1,9},{5... | collective-permute-start | bytes 860168 | tf_op jit(solution)/shard_map/ppermute | solution.py:434
  20.4 3.4 %solve_part.3 = (f32[1680,128]{1,0:T(8,128)S(1)}, f32[1680,128]{1,0:T(8,128)S(1)}, f32[1680,128]{1,0:T(8,128)S(1)}, f32[1680,128]{1,0:T(8,128)S(1)}) custom-call(bf16[1,560,128]{2,1,0:T(8,128)(2,1)S(1)} %pack_band.1.refs_0_, bf16[1,560,128]{2,1,0:T(8,128)(2,1)S(1)} %collective-permute-done.1.refs_1_, ...), custom_call_target="tpu_custom_call" | custom-call | flops 4000000000 | bytes 20000000 | tf_op jit(solution)/shard_map/solve_part/pallas_call | solution.py:487
  23.8 0.1 collective-permute-done.6.refs_5_
  23.9 1.0 %collective-permute-done.7.refs_6_ = bf16[2,560,128]{2,1,0:T(8,128)(2,1)S(1)} collective-permute-done((bf16[2,560,128]{2,1,0:T(8,128)(2,1)S(1)}, bf16[2,560,128]{2,1,0:T(8,128)(2,1)S(1)}, u32[]{:S(2)}, u32[]{:S(2)}) %collective-permute-start.7) | collective-permute-done | bytes 286752 | tf_op jit(solution)/shard_map/ppermute | solution.py:434
  25.0 1.1 %collective-permute-done.8.refs_7_ = bf16[2,560,128]{2,1,0:T(8,128)(2,1)S(1)} collective-permute-done((bf16[2,560,128]{2,1,0:T(8,128)(2,1)S(1)}, bf16[2,560,128]{2,1,0:T(8,128)(2,1)S(1)}, u32[]{:S(2)}, u32[]{:S(2)}) %collective-permute-start.8) | collective-permute-done | bytes 286752 | tf_op jit(solution)/shard_map/ppermute | solution.py:434
  26.1 0.6 %collective-permute-start.9 = (bf16[1,560,128]{2,1,0:T(8,128)(2,1)S(1)}, bf16[1,560,128]{2,1,0:T(8,128)(2,1)S(1)}, u32[]{:S(2)}, u32[]{:S(2)}) collective-permute-start(bf16[1,560,128]{2,1,0:T(8,128)(2,1)S(1)} %slice.6), channel_id=1, source_target_pairs={{0,2},{1,3},{2,0},{3,1},{4,6},{5,7},{6,4},{7,5},{8,10},{9,11},{10,... | collective-permute-start | bytes 430088 | tf_op jit(solution)/shard_map/ppermute | solution.py:434
  26.7 0.8 %collective-permute-start.10 = (bf16[1,560,128]{2,1,0:T(8,128)(2,1)S(1)}, bf16[1,560,128]{2,1,0:T(8,128)(2,1)S(1)}, u32[]{:S(2)}, u32[]{:S(2)}) collective-permute-start(bf16[1,560,128]{2,1,0:T(8,128)(2,1)S(1)} %slice.7), channel_id=1, source_target_pairs={{0,4},{4,0},{8,12},{12,8},{16,20},{20,16},{24,28},{28,24},{1,5},{5... | collective-permute-start | bytes 430088 | tf_op jit(solution)/shard_map/ppermute | solution.py:434
  27.6 1.5 %collective-permute-start.11 = (bf16[2,560,128]{2,1,0:T(8,128)(2,1)S(1)}, bf16[2,560,128]{2,1,0:T(8,128)(2,1)S(1)}, u32[]{:S(2)}, u32[]{:S(2)}) collective-permute-start(bf16[2,560,128]{2,1,0:T(8,128)(2,1)S(1)} %collective-permute-done.7.refs_6_), channel_id=1, source_target_pairs={{0,8},{4,12},{8,0},{12,4},{16,24},{20,28},{24,16},{28,20},{1,9},{5... | collective-permute-start | bytes 860168 | tf_op jit(solution)/shard_map/ppermute | solution.py:434
  29.0 2.3 %collective-permute-done.9.refs_8_ = bf16[1,560,128]{2,1,0:T(8,128)(2,1)S(1)} collective-permute-done((bf16[1,560,128]{2,1,0:T(8,128)(2,1)S(1)}, bf16[1,560,128]{2,1,0:T(8,128)(2,1)S(1)}, u32[]{:S(2)}, u32[]{:S(2)}) %collective-permute-start.9) | collective-permute-done | bytes 143392 | tf_op jit(solution)/shard_map/ppermute | solution.py:434
  31.3 0.6 %collective-permute-start.12 = (bf16[1,560,128]{2,1,0:T(8,128)(2,1)S(1)}, bf16[1,560,128]{2,1,0:T(8,128)(2,1)S(1)}, u32[]{:S(2)}, u32[]{:S(2)}) collective-permute-start(bf16[1,560,128]{2,1,0:T(8,128)(2,1)S(1)} %collective-permute-done.9.refs_8_), channel_id=1, source_target_pairs={{0,4},{4,0},{8,12},{12,8},{16,20},{20,16},{24,28},{28,24},{1,5},{5... | collective-permute-start | bytes 430088 | tf_op jit(solution)/shard_map/ppermute | solution.py:434
  31.9 1.5 %collective-permute-done.10.refs_9_ = bf16[1,560,128]{2,1,0:T(8,128)(2,1)S(1)} collective-permute-done((bf16[1,560,128]{2,1,0:T(8,128)(2,1)S(1)}, bf16[1,560,128]{2,1,0:T(8,128)(2,1)S(1)}, u32[]{:S(2)}, u32[]{:S(2)}) %collective-permute-start.10) | collective-permute-done | bytes 143392 | tf_op jit(solution)/shard_map/ppermute | solution.py:434
  33.4 5.9 %solve_part.4 = (f32[1680,128]{1,0:T(8,128)S(1)}, f32[1680,128]{1,0:T(8,128)S(1)}) custom-call(bf16[1,560,128]{2,1,0:T(8,128)(2,1)S(1)} %pack_band.1.refs_0_, bf16[1,560,128]{2,1,0:T(8,128)(2,1)S(1)} %collective-permute-done.1.refs_1_, bf16[1,560,128]{2,1,0:T(8,128)(2,1)S(1)} %collective-permute-done.2.refs_2_, ...), custom_call_target="tpu_custom_call" | custom-call | flops 4000000000 | bytes 20000000 | tf_op jit(solution)/shard_map/solve_part/pallas_call | solution.py:487
  39.3 5.3 %solve_part.5 = (f32[560,128]{1,0:T(8,128)S(1)}, f32[560,128]{1,0:T(8,128)S(1)}) custom-call(bf16[1,560,128]{2,1,0:T(8,128)(2,1)S(1)} %pack_band.1.refs_0_, bf16[1,560,128]{2,1,0:T(8,128)(2,1)S(1)} %collective-permute-done.1.refs_1_, bf16[1,560,128]{2,1,0:T(8,128)(2,1)S(1)} %collective-permute-done.2.refs_2_, ...), custom_call_target="tpu_custom_call" | custom-call | flops 4000000000 | bytes 20000000 | tf_op jit(solution)/shard_map/solve_part/pallas_call | solution.py:487
  44.6 0.1 collective-permute-start.13
  44.7 1.6 %collective-permute-done.13.part_ref = f32[560,128]{1,0:T(8,128)S(1)} collective-permute-done((f32[560,128]{1,0:T(8,128)S(1)}, f32[560,128]{1,0:T(8,128)S(1)}, u32[]{:S(2)}, u32[]{:S(2)}) %collective-permute-start.13) | collective-permute-done | bytes 286752 | tf_op jit(solution)/shard_map/ppermute | solution.py:434
  46.2 1.2 %add_parts.1 = f32[1,64000]{1,0:T(1,128)} custom-call(f32[560,128]{1,0:T(8,128)S(1)} %get-tuple-element.29.own_ref, f32[560,128]{1,0:T(8,128)S(1)} %collective-permute-done.13.part_ref), custom_call_target="tpu_custom_call" | custom-call | tf_op jit(solution)/shard_map/add_parts/pallas_call | solution.py:458
  (23 shorter events, 0.1 us)
Async XLA Ops:
  1.5 1.3 %collective-permute-start = (s32[1,8,2]{2,1,0:T(8,128)S(1)}, s32[1,8,2]{2,1,0:T(8,128)S(1)}, u32[]{:S(2)}, u32[]{:S(2)}) collective-permute-start(s32[1,8,2]{2,1,0:T(8,128)S(1)} %broadcast_select_fusion.rest_0_), channel_id=1, source_target_pairs={{0,1},{1,0},{2,3},{3,2},{4,5},{5,4},{6,7},{7,6},{8,9},{9,8},{10,11... | collective-permute-start | bytes 200 | tf_op jit(solution)/shard_map/ppermute | solution.py:434
  2.8 0.9 %copy-start = (bf16[1,64000]{1,0:T(2,128)(2,1)S(1)}, bf16[1,64000]{1,0:T(2,128)(2,1)}, u32[]{:S(2)}) copy-start(bf16[1,64000]{1,0:T(2,128)(2,1)} %band_ref.1) | copy-start | bytes 384004
  3.7 16.6 %copy-start.5 = (bf16[128,384]{1,0:T(8,128)(2,1)S(1)}, bf16[128,384]{1,0:T(8,128)(2,1)}, u32[]{:S(2)}) copy-start(bf16[128,384]{1,0:T(8,128)(2,1)} %constant.17.clone.refs_7_.refs_12_.refs_14_) | copy-start | bytes 294916
  3.7 16.6 %copy-start.7 = (bf16[80,240]{1,0:T(8,128)(2,1)S(1)}, bf16[80,240]{1,0:T(8,128)(2,1)}, u32[]{:S(2)}) copy-start(bf16[80,240]{1,0:T(8,128)(2,1)} %constant.21.clone.refs_11_.refs_16_.refs_18_) | copy-start | bytes 115204
  4.2 16.2 %copy-start.1 = (f32[1600,128]{1,0:T(8,128)S(1)}, f32[1600,128]{1,0:T(8,128)}, u32[]{:S(2)}) copy-start(f32[1600,128]{1,0:T(8,128)} %constant.22.clone.refs_12_.refs_17_.refs_19_) | copy-start | bytes 2457604
  4.2 16.2 %copy-start.2 = (bf16[384,384]{1,0:T(8,128)(2,1)S(1)}, bf16[384,384]{1,0:T(8,128)(2,1)}, u32[]{:S(2)}) copy-start(bf16[384,384]{1,0:T(8,128)(2,1)} %constant.16.clone.refs_6_.refs_11_.refs_13_) | copy-start | bytes 884740
  4.2 16.2 %copy-start.3 = (bf16[256,256]{1,0:T(8,128)(2,1)S(1)}, bf16[256,256]{1,0:T(8,128)(2,1)}, u32[]{:S(2)}) copy-start(bf16[256,256]{1,0:T(8,128)(2,1)} %constant.18.clone.refs_8_.refs_13_.refs_15_) | copy-start | bytes 393220
  4.2 16.2 %copy-start.4 = (bf16[256,256]{1,0:T(8,128)(2,1)S(1)}, bf16[256,256]{1,0:T(8,128)(2,1)}, u32[]{:S(2)}) copy-start(bf16[256,256]{1,0:T(8,128)(2,1)} %constant.19.clone.refs_9_.refs_14_.refs_16_) | copy-start | bytes 393220
  4.2 16.2 %copy-start.6 = (bf16[80,240]{1,0:T(8,128)(2,1)S(1)}, bf16[80,240]{1,0:T(8,128)(2,1)}, u32[]{:S(2)}) copy-start(bf16[80,240]{1,0:T(8,128)(2,1)} %constant.20.clone.refs_10_.refs_15_.refs_17_) | copy-start | bytes 115204
  4.2 11.3 %collective-permute-start.1 = (bf16[1,560,128]{2,1,0:T(8,128)(2,1)S(1)}, bf16[1,560,128]{2,1,0:T(8,128)(2,1)S(1)}, u32[]{:S(2)}, u32[]{:S(2)}) collective-permute-start(bf16[1,560,128]{2,1,0:T(8,128)(2,1)S(1)} %pack_band.1.refs_0_), channel_id=1, source_target_pairs={{0,16},{4,20},{8,24},{12,28},{16,0},{20,4},{24,8},{28,12},{1,17},{... | collective-permute-start | bytes 430088 | tf_op jit(solution)/shard_map/ppermute | solution.py:434
  8.2 7.5 %collective-permute-start.2 = (bf16[1,560,128]{2,1,0:T(8,128)(2,1)S(1)}, bf16[1,560,128]{2,1,0:T(8,128)(2,1)S(1)}, u32[]{:S(2)}, u32[]{:S(2)}) collective-permute-start(bf16[1,560,128]{2,1,0:T(8,128)(2,1)S(1)} %pack_band.1.refs_0_), channel_id=1, source_target_pairs={{0,8},{4,12},{8,0},{12,4},{16,24},{20,28},{24,16},{28,20},{1,9},{5... | collective-permute-start | bytes 430088 | tf_op jit(solution)/shard_map/ppermute | solution.py:434
  9.8 5.9 %collective-permute-start.3 = (bf16[1,560,128]{2,1,0:T(8,128)(2,1)S(1)}, bf16[1,560,128]{2,1,0:T(8,128)(2,1)S(1)}, u32[]{:S(2)}, u32[]{:S(2)}) collective-permute-start(bf16[1,560,128]{2,1,0:T(8,128)(2,1)S(1)} %pack_band.1.refs_0_), channel_id=1, source_target_pairs={{0,4},{4,0},{8,12},{12,8},{16,20},{20,16},{24,28},{28,24},{1,5},{5... | collective-permute-start | bytes 430088 | tf_op jit(solution)/shard_map/ppermute | solution.py:434
  11.3 5.1 %collective-permute-start.4 = (bf16[1,560,128]{2,1,0:T(8,128)(2,1)S(1)}, bf16[1,560,128]{2,1,0:T(8,128)(2,1)S(1)}, u32[]{:S(2)}, u32[]{:S(2)}) collective-permute-start(bf16[1,560,128]{2,1,0:T(8,128)(2,1)S(1)} %pack_band.1.refs_0_), channel_id=1, source_target_pairs={{0,2},{1,3},{2,0},{3,1},{4,6},{5,7},{6,4},{7,5},{8,10},{9,11},{10,... | collective-permute-start | bytes 430088 | tf_op jit(solution)/shard_map/ppermute | solution.py:434
  12.8 7.5 %collective-permute-start.5 = (bf16[1,560,128]{2,1,0:T(8,128)(2,1)S(1)}, bf16[1,560,128]{2,1,0:T(8,128)(2,1)S(1)}, u32[]{:S(2)}, u32[]{:S(2)}) collective-permute-start(bf16[1,560,128]{2,1,0:T(8,128)(2,1)S(1)} %pack_band.1.refs_0_), channel_id=1, source_target_pairs={{0,1},{1,0},{2,3},{3,2},{4,5},{5,4},{6,7},{7,6},{8,9},{9,8},{10,11... | collective-permute-start | bytes 430088 | tf_op jit(solution)/shard_map/ppermute | solution.py:434
  16.5 7.4 %collective-permute-start.6 = (bf16[2,560,128]{2,1,0:T(8,128)(2,1)S(1)}, bf16[2,560,128]{2,1,0:T(8,128)(2,1)S(1)}, u32[]{:S(2)}, u32[]{:S(2)}) collective-permute-start(bf16[2,560,128]{2,1,0:T(8,128)(2,1)S(1)} %get-tuple-element.33), channel_id=1, source_target_pairs={{0,2},{1,3},{2,0},{3,1},{4,6},{5,7},{6,4},{7,5},{8,10},{9,11},{10,... | collective-permute-start | bytes 860168 | tf_op jit(solution)/shard_map/ppermute | solution.py:434
  18.0 6.9 %collective-permute-start.7 = (bf16[2,560,128]{2,1,0:T(8,128)(2,1)S(1)}, bf16[2,560,128]{2,1,0:T(8,128)(2,1)S(1)}, u32[]{:S(2)}, u32[]{:S(2)}) collective-permute-start(bf16[2,560,128]{2,1,0:T(8,128)(2,1)S(1)} %get-tuple-element.32), channel_id=1, source_target_pairs={{0,4},{4,0},{8,12},{12,8},{16,20},{20,16},{24,28},{28,24},{1,5},{5... | collective-permute-start | bytes 860168 | tf_op jit(solution)/shard_map/ppermute | solution.py:434
  18.9 7.2 %collective-permute-start.8 = (bf16[2,560,128]{2,1,0:T(8,128)(2,1)S(1)}, bf16[2,560,128]{2,1,0:T(8,128)(2,1)S(1)}, u32[]{:S(2)}, u32[]{:S(2)}) collective-permute-start(bf16[2,560,128]{2,1,0:T(8,128)(2,1)S(1)} %get-tuple-element.31), channel_id=1, source_target_pairs={{0,8},{4,12},{8,0},{12,4},{16,24},{20,28},{24,16},{28,20},{1,9},{5... | collective-permute-start | bytes 860168 | tf_op jit(solution)/shard_map/ppermute | solution.py:434
  26.1 5.2 %collective-permute-start.9 = (bf16[1,560,128]{2,1,0:T(8,128)(2,1)S(1)}, bf16[1,560,128]{2,1,0:T(8,128)(2,1)S(1)}, u32[]{:S(2)}, u32[]{:S(2)}) collective-permute-start(bf16[1,560,128]{2,1,0:T(8,128)(2,1)S(1)} %slice.6), channel_id=1, source_target_pairs={{0,2},{1,3},{2,0},{3,1},{4,6},{5,7},{6,4},{7,5},{8,10},{9,11},{10,... | collective-permute-start | bytes 430088 | tf_op jit(solution)/shard_map/ppermute | solution.py:434
  26.7 6.6 %collective-permute-start.10 = (bf16[1,560,128]{2,1,0:T(8,128)(2,1)S(1)}, bf16[1,560,128]{2,1,0:T(8,128)(2,1)S(1)}, u32[]{:S(2)}, u32[]{:S(2)}) collective-permute-start(bf16[1,560,128]{2,1,0:T(8,128)(2,1)S(1)} %slice.7), channel_id=1, source_target_pairs={{0,4},{4,0},{8,12},{12,8},{16,20},{20,16},{24,28},{28,24},{1,5},{5... | collective-permute-start | bytes 430088 | tf_op jit(solution)/shard_map/ppermute | solution.py:434
  27.6 11.7 %collective-permute-start.11 = (bf16[2,560,128]{2,1,0:T(8,128)(2,1)S(1)}, bf16[2,560,128]{2,1,0:T(8,128)(2,1)S(1)}, u32[]{:S(2)}, u32[]{:S(2)}) collective-permute-start(bf16[2,560,128]{2,1,0:T(8,128)(2,1)S(1)} %collective-permute-done.7.refs_6_), channel_id=1, source_target_pairs={{0,8},{4,12},{8,0},{12,4},{16,24},{20,28},{24,16},{28,20},{1,9},{5... | collective-permute-start | bytes 860168 | tf_op jit(solution)/shard_map/ppermute | solution.py:434
  31.3 8.0 %collective-permute-start.12 = (bf16[1,560,128]{2,1,0:T(8,128)(2,1)S(1)}, bf16[1,560,128]{2,1,0:T(8,128)(2,1)S(1)}, u32[]{:S(2)}, u32[]{:S(2)}) collective-permute-start(bf16[1,560,128]{2,1,0:T(8,128)(2,1)S(1)} %collective-permute-done.9.refs_8_), channel_id=1, source_target_pairs={{0,4},{4,0},{8,12},{12,8},{16,20},{20,16},{24,28},{28,24},{1,5},{5... | collective-permute-start | bytes 430088 | tf_op jit(solution)/shard_map/ppermute | solution.py:434
  44.6 1.6 %collective-permute-start.13 = (f32[560,128]{1,0:T(8,128)S(1)}, f32[560,128]{1,0:T(8,128)S(1)}, u32[]{:S(2)}, u32[]{:S(2)}) collective-permute-start(f32[560,128]{1,0:T(8,128)S(1)} %get-tuple-element.30), channel_id=1, source_target_pairs={{0,1},{1,0},{2,3},{3,2},{4,5},{5,4},{6,7},{7,6},{8,9},{9,8},{10,11... | collective-permute-start | bytes 860168 | tf_op jit(solution)/shard_map/ppermute | solution.py:434
